TPU v7x, 512 devices: a whole 4x4x16 slice. The times are simulated.
512 devices in a mesh: lat: 32 (over y, z_hi, x), lon: 16 (over z_lo, core).
Axes of the slice: x: 4, y: 4, z: 16 (z_hi: 2, z_lo: 8; z = z_hi * 8 + z_lo), core: 2. Of those that a mesh axis runs over, the one named last changes fastest.
Arguments:
- members: bfloat16 [40, 1024, 4096], P(None, 'lat', 'lon'), may hold values from -6 to 6
- support: int32 [1024], replicated, may hold values from 32 to 2048, as said below
Outputs:
- localized: float32 [40, 1024, 4096], P(None, 'lat', 'lon')
Inputs may be any that keep to these rules, and one draw needn't show every extreme that they name: For rows r with 64 <= r < 960, support[r] <= 256; support[r] >= 32 everywhere.
All inputs are finite; a program needn't handle non-finite values.
Results may differ from a plain program's by a relative error of at most 0.0045.
Values may be sent and summed in bfloat16 or wider, within the bound.
No kernel may reach another device: no remote copies, remote signals or barrier semaphores. Data moves between devices by JAX's collectives and lax.ppermute only.
A program may use at most 64 MiB of HBM per device.

v0:
```python
import math

import jax
import jax.numpy as jnp
from jax import lax
from jax.sharding import PartitionSpec as P

HALF_LAT = 24


def with_halo(block, sides, width):
    for axis, dim in sides:
        count = lax.axis_size(axis)
        forward = [(i, i + 1) for i in range(count - 1)]
        backward = [(target, source) for source, target in forward]
        low = lax.ppermute(
            lax.slice_in_dim(block, block.shape[dim] - width, None, axis=dim), axis, forward
        )
        high = lax.ppermute(lax.slice_in_dim(block, 0, width, axis=dim), axis, backward)
        block = jnp.concatenate([low, block, high], axis=dim)
    return block


def row_scale(widths, nlon_all):
    cycle_cols = jnp.arange(nlon_all)
    distance = jnp.minimum(cycle_cols, nlon_all - cycle_cols).astype(jnp.float32)[None, :]
    width_f = widths.astype(jnp.float32)[:, None]
    weights_raw = jnp.where(
        distance <= width_f, jnp.exp(-2.0 * distance * distance / (width_f * width_f)), 0.0
    )
    return 1.0 / jnp.sqrt(jnp.sum(weights_raw * weights_raw, axis=1))


def group_product(blocks, widths, in_cols, out_cols, nlon_all):
    offset_cols = (in_cols[:, None] - out_cols[None, :]) % nlon_all
    distance = jnp.minimum(offset_cols, nlon_all - offset_cols).astype(jnp.float32)[None]
    width_f = widths.astype(jnp.float32)[:, None, None]
    weights_raw = jnp.where(
        distance <= width_f, jnp.exp(-2.0 * distance * distance / (width_f * width_f)), 0.0
    )
    kernel = (weights_raw * row_scale(widths, nlon_all)[:, None, None]).astype(jnp.bfloat16)
    return jnp.einsum("mrj,rjc->mrc", blocks, kernel, preferred_element_type=jnp.float32)


def convolve(data, widths, in_cols, out_cols, nlon_all):
    member_count, row_count, span_cols = data.shape
    group_rows = math.gcd(row_count, 4)
    groups = row_count // group_rows
    blocks = data.reshape(member_count, groups, group_rows, span_cols).transpose(1, 0, 2, 3)
    width_sets = widths.reshape(groups, group_rows)

    def group_step(group_pair):
        return group_product(group_pair[0], group_pair[1], in_cols, out_cols, nlon_all)

    result = lax.map(group_step, (blocks, width_sets))
    return result.transpose(1, 0, 2, 3).reshape(member_count, row_count, out_cols.shape[0])


def body(members, support):
    member_count, lat_rows, lon_cols = members.shape
    lat_count = lax.axis_size("lat")
    lon_count = lax.axis_size("lon")
    nlon_all = lon_count * lon_cols
    lat_index = lax.axis_index("lat")
    lon_index = lax.axis_index("lon")
    out_cols = lon_index * lon_cols + jnp.arange(lon_cols)
    widths = lax.dynamic_slice_in_dim(support, lat_index * lat_rows, lat_rows)
    piece = lax.all_gather(members, "lon", axis=2, tiled=True)
    in_cols = jnp.arange(piece.shape[2])
    along = convolve(piece, widths, in_cols, out_cols, nlon_all).astype(jnp.bfloat16)
    half_rows = HALF_LAT
    widened = with_halo(along, (("lat", 1),), half_rows)
    source_rows = jnp.arange(lat_rows + 2 * half_rows)
    own_rows = jnp.arange(lat_rows)
    offsets_band = (source_rows[:, None] - half_rows - own_rows[None, :]).astype(jnp.float32)
    banded = jnp.where(
        jnp.abs(offsets_band) <= half_rows,
        jnp.exp(-2.0 * offsets_band * offsets_band / (half_rows * half_rows)),
        0.0,
    ).astype(jnp.bfloat16)
    global_rows = lat_index * lat_rows + own_rows
    offsets = jnp.arange(-half_rows, half_rows + 1)
    offset_f = offsets.astype(jnp.float32)
    values = jnp.exp(-2.0 * offset_f * offset_f / (half_rows * half_rows))
    reached = global_rows[:, None] + offsets[None, :]
    inside = (reached >= 0) & (reached < lat_count * lat_rows)
    lat_norms = 1.0 / jnp.sqrt(jnp.sum(jnp.where(inside, (values * values)[None, :], 0.0), axis=1))
    smoothed = jnp.einsum("mjc,jr->mrc", widened, banded, preferred_element_type=jnp.float32)
    return smoothed * lat_norms[None, :, None]


def solution(mesh):
    placed = (P(None, "lat", "lon"), P())
    return jax.shard_map(
        body, mesh=mesh, in_specs=placed, out_specs=P(None, "lat", "lon"), check_vma=False
    )
```

profile of v0, /device:TPU:15, one launch (start us, length us, event | category | flops | bytes accessed | tf_op | source)
XLA Modules:
  0.0 311.8 jit_solution(1670027697714470331)
XLA Ops:
  8.1 139.9 %all-gather.2.cloned.1.call-done = bf16[40,32,4096]{2,1,0:T(8,128)(2,1)} async-done(((bf16[40,32,256]{2,1,0:T(8,128)(2,1)}), bf16[40,32,4096]{2,1,0:T(8,128)(2,1)}) %all-gather.2.cloned.1.call-update) | async-done | bytes 10485776 | tf_op jit(solution)/shard_map/all_gather | solution.py:68
  148.0 13.7 %copy.7 = bf16[40,32,4096]{2,0,1:T(8,128)(2,1)} copy(bf16[40,32,4096]{2,1,0:T(8,128)(2,1)} %all-gather.2.cloned.1.call-done) | data formatting | bytes 20971520 | tf_op jit(solution)/shard_map/all_gather | solution.py:68
  161.7 82.7 %while.13 = (s32[]{:T(128)}, bf16[8,40,4,256]{3,1,2,0:T(8,128)(2,1)S(1)}, s32[8,4]{1,0:T(8,128)S(1)}, bf16[8,40,4,4096]{3,1,2,0:T(8,128)(2,1)}, s32[]{:T(128)}, /*index=5*/s32[]{:T(128)}) while((s32[]{:T(128)}, bf16[8,40,4,256]{3,1,2,0:T(8,128)(2,1)S(1)}, s32[8,4]{1,0:T(8,128)S(1)}, bf16[8,40,4,4096]{3,1,2,0:T(8,128)(2,1)}, ...), condition=%wide.region_2.3_spmd.clone, body=%wide.region_0.2_spmd.clone.sunk | while | flops 390185216 | bytes 18323156 | solution.py:55
  162.0 2.3 fusion.81
  164.3 2.6 multiply_multiply_fusion.7
  166.9 5.1 %fusion.82 = bf16[8,40,4,256]{3,1,2,0:T(8,128)(2,1)S(1)} fusion(bf16[8,40,4,256]{3,1,2,0:T(8,128)(2,1)S(1)} %get-tuple-element.154, s32[]{:T(128)S(6)} %copy.13, bf16[8,40,4,4096]{3,1,2,0:T(8,128)(2,1)} %get-tuple-element.162, f32[4]{0:T(128)S(1)} %sqrt.9, f32[4]{0:T(128)S(1)} %get-tuple-element.145, f32[4096,256]{1,0:T(8,128)S(1)} %multiply_multiply_fusion.7, ...), kind=kOutput, calls=%fused_computation.21.clone.1 | convolution fusion | flops 356515840 | bytes 9865728 | tf_op jit(solution)/shard_map/while/body/eval_jaxpr/mrj,rjc->mrc/dot_general | solution.py:42
  172.3 2.3 fusion.81
  174.6 2.6 multiply_multiply_fusion.7
  177.2 5.1 %fusion.82 = bf16[8,40,4,256]{3,1,2,0:T(8,128)(2,1)S(1)} fusion(bf16[8,40,4,256]{3,1,2,0:T(8,128)(2,1)S(1)} %get-tuple-element.154, s32[]{:T(128)S(6)} %copy.13, bf16[8,40,4,4096]{3,1,2,0:T(8,128)(2,1)} %get-tuple-element.162, f32[4]{0:T(128)S(1)} %sqrt.9, f32[4]{0:T(128)S(1)} %get-tuple-element.145, f32[4096,256]{1,0:T(8,128)S(1)} %multiply_multiply_fusion.7, ...), kind=kOutput, calls=%fused_computation.21.clone.1 | convolution fusion | flops 356515840 | bytes 9865728 | tf_op jit(solution)/shard_map/while/body/eval_jaxpr/mrj,rjc->mrc/dot_general | solution.py:42
  182.7 2.3 fusion.81
  185.0 2.6 multiply_multiply_fusion.7
  187.6 5.1 %fusion.82 = bf16[8,40,4,256]{3,1,2,0:T(8,128)(2,1)S(1)} fusion(bf16[8,40,4,256]{3,1,2,0:T(8,128)(2,1)S(1)} %get-tuple-element.154, s32[]{:T(128)S(6)} %copy.13, bf16[8,40,4,4096]{3,1,2,0:T(8,128)(2,1)} %get-tuple-element.162, f32[4]{0:T(128)S(1)} %sqrt.9, f32[4]{0:T(128)S(1)} %get-tuple-element.145, f32[4096,256]{1,0:T(8,128)S(1)} %multiply_multiply_fusion.7, ...), kind=kOutput, calls=%fused_computation.21.clone.1 | convolution fusion | flops 356515840 | bytes 9865728 | tf_op jit(solution)/shard_map/while/body/eval_jaxpr/mrj,rjc->mrc/dot_general | solution.py:42
  193.0 2.3 fusion.81
  195.3 2.6 multiply_multiply_fusion.7
  197.9 5.1 %fusion.82 = bf16[8,40,4,256]{3,1,2,0:T(8,128)(2,1)S(1)} fusion(bf16[8,40,4,256]{3,1,2,0:T(8,128)(2,1)S(1)} %get-tuple-element.154, s32[]{:T(128)S(6)} %copy.13, bf16[8,40,4,4096]{3,1,2,0:T(8,128)(2,1)} %get-tuple-element.162, f32[4]{0:T(128)S(1)} %sqrt.9, f32[4]{0:T(128)S(1)} %get-tuple-element.145, f32[4096,256]{1,0:T(8,128)S(1)} %multiply_multiply_fusion.7, ...), kind=kOutput, calls=%fused_computation.21.clone.1 | convolution fusion | flops 356515840 | bytes 9865728 | tf_op jit(solution)/shard_map/while/body/eval_jaxpr/mrj,rjc->mrc/dot_general | solution.py:42
  203.3 2.3 fusion.81
  205.7 2.6 multiply_multiply_fusion.7
  208.2 5.1 %fusion.82 = bf16[8,40,4,256]{3,1,2,0:T(8,128)(2,1)S(1)} fusion(bf16[8,40,4,256]{3,1,2,0:T(8,128)(2,1)S(1)} %get-tuple-element.154, s32[]{:T(128)S(6)} %copy.13, bf16[8,40,4,4096]{3,1,2,0:T(8,128)(2,1)} %get-tuple-element.162, f32[4]{0:T(128)S(1)} %sqrt.9, f32[4]{0:T(128)S(1)} %get-tuple-element.145, f32[4096,256]{1,0:T(8,128)S(1)} %multiply_multiply_fusion.7, ...), kind=kOutput, calls=%fused_computation.21.clone.1 | convolution fusion | flops 356515840 | bytes 9865728 | tf_op jit(solution)/shard_map/while/body/eval_jaxpr/mrj,rjc->mrc/dot_general | solution.py:42
  213.7 2.3 fusion.81
  216.0 2.6 multiply_multiply_fusion.7
  218.6 5.1 %fusion.82 = bf16[8,40,4,256]{3,1,2,0:T(8,128)(2,1)S(1)} fusion(bf16[8,40,4,256]{3,1,2,0:T(8,128)(2,1)S(1)} %get-tuple-element.154, s32[]{:T(128)S(6)} %copy.13, bf16[8,40,4,4096]{3,1,2,0:T(8,128)(2,1)} %get-tuple-element.162, f32[4]{0:T(128)S(1)} %sqrt.9, f32[4]{0:T(128)S(1)} %get-tuple-element.145, f32[4096,256]{1,0:T(8,128)S(1)} %multiply_multiply_fusion.7, ...), kind=kOutput, calls=%fused_computation.21.clone.1 | convolution fusion | flops 356515840 | bytes 9865728 | tf_op jit(solution)/shard_map/while/body/eval_jaxpr/mrj,rjc->mrc/dot_general | solution.py:42
  224.0 2.3 fusion.81
  226.3 2.6 multiply_multiply_fusion.7
  228.9 5.1 %fusion.82 = bf16[8,40,4,256]{3,1,2,0:T(8,128)(2,1)S(1)} fusion(bf16[8,40,4,256]{3,1,2,0:T(8,128)(2,1)S(1)} %get-tuple-element.154, s32[]{:T(128)S(6)} %copy.13, bf16[8,40,4,4096]{3,1,2,0:T(8,128)(2,1)} %get-tuple-element.162, f32[4]{0:T(128)S(1)} %sqrt.9, f32[4]{0:T(128)S(1)} %get-tuple-element.145, f32[4096,256]{1,0:T(8,128)S(1)} %multiply_multiply_fusion.7, ...), kind=kOutput, calls=%fused_computation.21.clone.1 | convolution fusion | flops 356515840 | bytes 9865728 | tf_op jit(solution)/shard_map/while/body/eval_jaxpr/mrj,rjc->mrc/dot_general | solution.py:42
  234.3 2.3 fusion.81
  236.7 2.6 multiply_multiply_fusion.7
  239.2 5.1 %fusion.82 = bf16[8,40,4,256]{3,1,2,0:T(8,128)(2,1)S(1)} fusion(bf16[8,40,4,256]{3,1,2,0:T(8,128)(2,1)S(1)} %get-tuple-element.154, s32[]{:T(128)S(6)} %copy.13, bf16[8,40,4,4096]{3,1,2,0:T(8,128)(2,1)} %get-tuple-element.162, f32[4]{0:T(128)S(1)} %sqrt.9, f32[4]{0:T(128)S(1)} %get-tuple-element.145, f32[4096,256]{1,0:T(8,128)S(1)} %multiply_multiply_fusion.7, ...), kind=kOutput, calls=%fused_computation.21.clone.1 | convolution fusion | flops 356515840 | bytes 9865728 | tf_op jit(solution)/shard_map/while/body/eval_jaxpr/mrj,rjc->mrc/dot_general | solution.py:42
  244.6 6.1 %collective-permute-start = (bf16[40,24,256]{2,1,0:T(8,128)(2,1)S(1)}, bf16[40,24,256]{2,1,0:T(8,128)(2,1)S(1)}, u32[]{:S(2)}, u32[]{:S(2)}) collective-permute-start(bf16[40,24,256]{2,1,0:T(8,128)(2,1)S(1)} %get-tuple-element.110), channel_id=1, source_target_pairs={{0,16},{16,32},{32,48},{48,64},{64,80},{80,96},{96,112},{112,128},... | collective-permute-start | bytes 1474568 | tf_op jit(solution)/shard_map/ppermute | solution.py:16
  250.7 1.9 collective-permute-start.1
  252.9 35.5 %collective-permute-done = bf16[40,24,256]{2,1,0:T(8,128)(2,1)S(1)} collective-permute-done((bf16[40,24,256]{2,1,0:T(8,128)(2,1)S(1)}, bf16[40,24,256]{2,1,0:T(8,128)(2,1)S(1)}, u32[]{:S(2)}, u32[]{:S(2)}) %collective-permute-start) | collective-permute-done | bytes 491552 | tf_op jit(solution)/shard_map/ppermute | solution.py:16
  288.4 15.2 %collective-permute-done.1 = bf16[40,24,256]{2,1,0:T(8,128)(2,1)S(1)} collective-permute-done((bf16[40,24,256]{2,1,0:T(8,128)(2,1)S(1)}, bf16[40,24,256]{2,1,0:T(8,128)(2,1)S(1)}, u32[]{:S(2)}, u32[]{:S(2)}) %collective-permute-start.1) | collective-permute-done | bytes 491552 | tf_op jit(solution)/shard_map/ppermute | solution.py:19
  303.6 1.4 fusion.43
  (61 shorter events, 4.1 us)
Async XLA Ops:
  6.5 141.5 %all-gather.2.cloned.1.call-start = ((), (), s32[]{:S(2)}) async-start(), calls=%async_computation | async-start | bytes 11141120 | tf_op jit(solution)/shard_map/all_gather | solution.py:68
  244.6 43.8 %collective-permute-start = (bf16[40,24,256]{2,1,0:T(8,128)(2,1)S(1)}, bf16[40,24,256]{2,1,0:T(8,128)(2,1)S(1)}, u32[]{:S(2)}, u32[]{:S(2)}) collective-permute-start(bf16[40,24,256]{2,1,0:T(8,128)(2,1)S(1)} %get-tuple-element.110), channel_id=1, source_target_pairs={{0,16},{16,32},{32,48},{48,64},{64,80},{80,96},{96,112},{112,128},... | collective-permute-start | bytes 1474568 | tf_op jit(solution)/shard_map/ppermute | solution.py:16
  250.7 52.8 %collective-permute-start.1 = (bf16[40,24,256]{2,1,0:T(8,128)(2,1)S(1)}, bf16[40,24,256]{2,1,0:T(8,128)(2,1)S(1)}, u32[]{:S(2)}, u32[]{:S(2)}) collective-permute-start(bf16[40,24,256]{2,1,0:T(8,128)(2,1)S(1)} %get-tuple-element.111), channel_id=1, source_target_pairs={{16,0},{32,16},{48,32},{64,48},{80,64},{96,80},{112,96},{128,112},... | collective-permute-start | bytes 1474568 | tf_op jit(solution)/shard_map/ppermute | solution.py:19
Sparse Core Ops, SparseCore 0:
  9.4 138.6 all-gather.1
where the time goes:
time: 312 us
  waiting for transfers between devices  191 us (61%)
  matrix products  42.4 us (14%)
  other arithmetic  41.3 us (13%)
  local copies, waits for them, and re-layouts  14.8 us (5%)
  between operations  13.5 us (4%)
  starting transfers between devices  8.05 us (3%)
    all_gather x1, waiting for transfers between devices, body(): piece = lax.all_gather(members, 'lon', axis=2, tiled=True)  140 us
    dot_general x8, matrix products, group_product(): jnp.einsum('mrj,rjc->mrc', blocks, kernel, preferred_element_type=jnp.flo...  41 us
    ppermute x1, waiting for transfers between devices, with_halo(): lax.ppermute(lax.slice_in_dim(block, block.shape[dim] - width, None, axis...  35.5 us
    mul x8, other arithmetic, group_product(): -2.0 * distance * distance / (width_f * width_f)  20.6 us
    convert_element_type x8, other arithmetic, group_product(): jnp.minimum(offset_cols, nlon_all - offset_cols).astype(jnp.float32)[None]  18.4 us
    ppermute x1, waiting for transfers between devices, with_halo(): lax.ppermute(lax.slice_in_dim(block, 0, width, axis=dim), axis, backward)  15.2 us
    all_gather x1, local copies, waits for them, and re-layouts, body(): piece = lax.all_gather(members, 'lon', axis=2, tiled=True)  13.7 us
  transfers between devices with their start and end apart: 3, of which 3 were waited for; matrix products, arithmetic and copies ran while one was open for 0% of the time, Pallas kernels for 0%

commit v1 on v0

v1 whole, which is shorter than its diff:
```python
import functools

import jax
import jax.numpy as jnp
from jax import lax
from jax.experimental import pallas as pl
from jax.experimental.pallas import tpu as pltpu
from jax.sharding import PartitionSpec as P

HALF_LAT = 24
POLAR = 64
X_RUN = 4
TILE = 128


def flat_pairs(lat_count, lon_count, target):
    pairs = []
    for lat in range(lat_count):
        for lon in range(lon_count):
            to = target(lat, lon)
            if to is not None and 0 <= to[0] < lat_count:
                pairs.append((lat * lon_count + lon, to[0] * lon_count + to[1] % lon_count))
    return pairs


def toeplitz(offset, square, falloff, scale, nlon_all=None):
    distance = jnp.abs(offset)
    if nlon_all is not None:
        distance = jnp.minimum(distance, nlon_all - distance)
    distance_sq = distance * distance
    raw = jnp.where(distance_sq <= square, jnp.exp(distance_sq * falloff), 0.0)
    return (raw * scale).astype(jnp.bfloat16)


def near_kernel(width_ref, scale_ref, left_ref, mid_ref, right_ref, out_ref):
    rows = mid_ref.shape[0]
    first = pl.program_id(0) * rows
    base = (
        lax.broadcasted_iota(jnp.int32, (TILE, TILE), 0)
        - lax.broadcasted_iota(jnp.int32, (TILE, TILE), 1)
    ).astype(jnp.float32)
    zero = jnp.zeros((TILE, TILE), jnp.bfloat16)
    for row in range(rows):
        width = width_ref[first + row]
        scale = scale_ref[first + row]
        square = width * width
        falloff = -2.0 / square
        t = {3: zero, -3: zero}
        for k in range(-2, 3):
            t[k] = toeplitz(base + float(k * TILE), square, falloff, scale)
        weights = jnp.concatenate(
            [jnp.concatenate([t[a - 2], t[a - 3]], axis=1) for a in range(6)], axis=0
        )
        data = jnp.concatenate([left_ref[row], mid_ref[row], right_ref[row]], axis=1)
        out_ref[row] = jnp.dot(data, weights, preferred_element_type=jnp.float32).astype(
            jnp.bfloat16
        )


def near_product(left, mid, right, widths, scales):
    rows, members, cols = mid.shape
    step = 8
    block = pl.BlockSpec((step, members, cols), lambda i: (i, 0, 0))
    smem = pl.BlockSpec(memory_space=pltpu.SMEM)
    return pl.pallas_call(
        near_kernel,
        grid=(rows // step,),
        in_specs=[smem, smem, block, block, block],
        out_specs=block,
        out_shape=jax.ShapeDtypeStruct(mid.shape, jnp.bfloat16),
        compiler_params=pltpu.CompilerParams(vmem_limit_bytes=48 * 1024 * 1024),
    )(widths, scales, left, mid, right)


def circle_kernel(blocks, width_ref, scale_ref, data_ref, out_ref, twice, total):
    size, cols = data_ref.shape[1:]
    span = size // blocks
    nlon_all = float(blocks * cols)
    base = (
        lax.broadcasted_iota(jnp.int32, (cols, cols), 0)
        - lax.broadcasted_iota(jnp.int32, (cols, cols), 1)
    ).astype(jnp.float32)
    for row in range(data_ref.shape[0]):
        twice[:size] = data_ref[row]
        twice[size:] = data_ref[row]
        width = width_ref[row]
        scale = scale_ref[row]
        square = width * width
        falloff = -2.0 / square
        total[...] = jnp.zeros_like(total)

        def step(k, carry):
            offset = base + (k * cols).astype(jnp.float32)
            weights = toeplitz(offset, square, falloff, scale, nlon_all)
            data = twice[pl.ds(pl.multiple_of(k * span, 16), size)]
            total[...] += jnp.dot(data, weights, preferred_element_type=jnp.float32)
            return carry

        lax.fori_loop(0, blocks, step, 0)
        out_ref[row] = total[...].astype(jnp.bfloat16)


def circle_product(data, widths, scales, blocks):
    rows, size, cols = data.shape
    smem = pl.BlockSpec(memory_space=pltpu.SMEM)
    vmem = pl.BlockSpec(memory_space=pltpu.VMEM)
    return pl.pallas_call(
        functools.partial(circle_kernel, blocks),
        in_specs=[smem, smem, vmem],
        out_specs=vmem,
        out_shape=jax.ShapeDtypeStruct(data.shape, jnp.bfloat16),
        scratch_shapes=[
            pltpu.VMEM((2 * size, cols), jnp.bfloat16),
            pltpu.VMEM((size, cols), jnp.float32),
        ],
        compiler_params=pltpu.CompilerParams(vmem_limit_bytes=48 * 1024 * 1024),
    )(widths, scales, data)


def row_scale(width_f, nlon_all):
    cycle_cols = jnp.arange(nlon_all)
    distance = jnp.minimum(cycle_cols, nlon_all - cycle_cols).astype(jnp.float32)[None, :]
    width_f = width_f[:, None]
    weights_raw = jnp.where(
        distance <= width_f, jnp.exp(-2.0 * distance * distance / (width_f * width_f)), 0.0
    )
    return 1.0 / jnp.sqrt(jnp.sum(weights_raw * weights_raw, axis=1))


def polar_along(data, widths, scales):
    rows, members, cols = data.shape
    lon_count = lax.axis_size("lon")
    own = rows // lon_count
    padded = -members % 16
    parts = data.reshape(lon_count, own, members, cols)
    parts = lax.all_to_all(parts, "lon", 0, 0)
    parts = jnp.pad(parts.transpose(1, 0, 2, 3), ((0, 0), (0, 0), (0, padded), (0, 0)))
    parts = parts.reshape(own, lon_count * (members + padded), cols)
    first = lax.axis_index("lon") * own
    result = circle_product(
        parts,
        lax.dynamic_slice_in_dim(widths, first, own),
        lax.dynamic_slice_in_dim(scales, first, own),
        lon_count,
    )
    result = result.reshape(own, lon_count, members + padded, cols)[:, :, :members]
    result = lax.all_to_all(result.transpose(1, 0, 2, 3), "lon", 0, 0)
    return result.reshape(rows, members, cols)


def lat_halo(along, lat_index, lat_count, lon_count):
    axes = ("lat", "lon")
    last, x = X_RUN - 1, lat_index % X_RUN
    pairs = functools.partial(flat_pairs, lat_count, lon_count)
    lower, upper = along[:HALF_LAT], along[-HALF_LAT:]
    far = lax.ppermute(
        jnp.where(x == last, upper, lower),
        axes,
        pairs(
            lambda lat, lon: (lat + 1, lon)
            if lat % X_RUN == last
            else ((lat - 1, lon) if lat % X_RUN == 0 else None)
        ),
    )
    low = lax.ppermute(
        upper, axes, pairs(lambda lat, lon: (lat + 1, lon) if lat % X_RUN != last else None)
    )
    high = lax.ppermute(
        lower, axes, pairs(lambda lat, lon: (lat - 1, lon) if lat % X_RUN != 0 else None)
    )
    return jnp.where(x == 0, far, low), jnp.where(x == last, far, high)


def body(members, support):
    member_count, lat_rows, lon_cols = members.shape
    lat_count = lax.axis_size("lat")
    lon_count = lax.axis_size("lon")
    nlon_all = lon_count * lon_cols
    nlat_all = lat_count * lat_rows
    lat_index = lax.axis_index("lat")
    axes = ("lat", "lon")

    def polar_of(lat):
        return (lat * lat_rows < POLAR) | ((lat + 1) * lat_rows > nlat_all - POLAR)

    pairs = functools.partial(flat_pairs, lat_count, lon_count)
    data = members.transpose(1, 0, 2)
    left = lax.ppermute(
        data, axes, pairs(lambda lat, lon: None if polar_of(lat) else (lat, lon + 1))
    )
    right = lax.ppermute(
        data, axes, pairs(lambda lat, lon: None if polar_of(lat) else (lat, lon - 1))
    )
    widths = lax.dynamic_slice_in_dim(support, lat_index * lat_rows, lat_rows).astype(jnp.float32)
    scales = row_scale(widths, nlon_all)
    along = lax.cond(
        polar_of(lat_index),
        lambda: polar_along(data, widths, scales),
        lambda: near_product(left, data, right, widths, scales),
    )

    low, high = lat_halo(along, lat_index, lat_count, lon_count)
    widened = jnp.concatenate([low, along, high], axis=0)

    half_rows = HALF_LAT
    source_rows = jnp.arange(lat_rows + 2 * half_rows)
    own_rows = jnp.arange(lat_rows)
    offsets_band = (source_rows[:, None] - half_rows - own_rows[None, :]).astype(jnp.float32)
    banded = jnp.where(
        jnp.abs(offsets_band) <= half_rows,
        jnp.exp(-2.0 * offsets_band * offsets_band / (half_rows * half_rows)),
        0.0,
    ).astype(jnp.bfloat16)
    global_rows = lat_index * lat_rows + own_rows
    offsets = jnp.arange(-half_rows, half_rows + 1)
    offset_f = offsets.astype(jnp.float32)
    values = jnp.exp(-2.0 * offset_f * offset_f / (half_rows * half_rows))
    reached = global_rows[:, None] + offsets[None, :]
    inside = (reached >= 0) & (reached < nlat_all)
    lat_norms = 1.0 / jnp.sqrt(jnp.sum(jnp.where(inside, (values * values)[None, :], 0.0), axis=1))
    smoothed = jnp.einsum("jmc,jr->mrc", widened, banded, preferred_element_type=jnp.float32)
    return smoothed * lat_norms[None, :, None]


def solution(mesh):
    placed = (P(None, "lat", "lon"), P())
    return jax.shard_map(
        body, mesh=mesh, in_specs=placed, out_specs=P(None, "lat", "lon"), check_vma=False
    )
```

time: 312 us -> 140 us (0.45)
  the two profiles are of different devices: /device:TPU:15 before, /device:TPU:1 now
where the time goes in v1:
time: 140 us; the launch traced here: 139 us
  blocking collectives  58.9 us (42%)
  waiting for transfers between devices  41.6 us (30%)
  starting transfers between devices  18.8 us (13%)
  Pallas kernels  11.8 us (8%)
  local copies, waits for them, and re-layouts  5.25 us (4%)
  other arithmetic  1.43 us (1%)
  matrix products  1.43 us (1%)
    all_to_all x1, blocking collectives, polar_along(): result = lax.all_to_all(result.transpose(1, 0, 2, 3), 'lon', 0, 0)  58.9 us
    all_to_all x1, waiting for transfers between devices, polar_along(): parts = lax.all_to_all(parts, 'lon', 0, 0)  30.6 us
    all_to_all x1, starting transfers between devices, polar_along(): parts = lax.all_to_all(parts, 'lon', 0, 0)  14.1 us
    pallas_call x1, Pallas kernels, circle_product(): pl.pallas_call(functools.partial(circle_kernel, blocks), in_specs=[smem,...  11.8 us
    ppermute x1, waiting for transfers between devices, lat_halo(): lax.ppermute(upper, axes, pairs(lambda lat, lon: (lat + 1, lon) if lat %...  7.15 us
    ppermute x1, waiting for transfers between devices, lat_halo(): lax.ppermute(lower, axes, pairs(lambda lat, lon: (lat - 1, lon) if lat %...  3.82 us
  transfers between devices with their start and end apart: 6, of which 3 were waited for; matrix products, arithmetic and copies ran while one was open for 2% of the time, Pallas kernels for 0%

profile of v1, /device:TPU:1, one launch (start us, length us, event | category | flops | bytes accessed | tf_op | source)
XLA Modules:
  0.0 139.3 jit_solution(9319243832541915765)
XLA Ops:
  0.0 2.3 %copy.37 = bf16[40,32,256]{2,0,1:T(8,128)(2,1)} copy(bf16[40,32,256]{2,1,0:T(8,128)(2,1)} %param.4) | data formatting | bytes 1310720 | tf_op args[0]
  2.3 0.7 collective-permute-start
  3.0 0.7 collective-permute-start.1
  3.7 0.8 fusion.36
  4.5 0.3 fusion.14
  4.8 0.0 collective-permute-done
  4.8 0.0 collective-permute-done.1
  4.8 117.1 %conditional.1 = (bf16[32,40,256]{2,1,0:T(8,128)(2,1)}, bf16[24,40,256]{2,0,1:T(8,128)(2,1)S(1)}, bf16[24,40,256]{2,0,1:T(8,128)(2,1)S(1)}) conditional(s32[]{:T(128)} %convert_element_type.35, (f32[32]{0:T(128)S(1)}, f32[32]{0:T(128)S(1)}, bf16[32,40,256]{2,1,0:T(8,128)(2,1)S(1)}, bf16[32,40,256]{2,1,0:T(8,128)(2,1)}, ...), branch_computations={%region_1.2_spmd, %region_2.3_spmd} | conditional | flops 6 | bytes 11272356 | solution.py:196
  4.9 14.1 %all-to-all-start = ((bf16[16,2,40,256]{3,2,1,0:T(8,128)(2,1)}), bf16[16,2,40,256]{3,2,1,0:T(8,128)(2,1)S(1)}, u32[]{:S(2)}, u32[]{:S(2)}) async-start(bf16[16,2,40,256]{3,2,1,0:T(8,128)(2,1)} %bitcast), calls=%async_computation | async-start | bytes 1310720 | tf_op jit(solution)/shard_map/cond/branch_1_fun/all_to_all | solution.py:136
  18.9 0.1 dynamic_slice.6.width_ref
  19.0 0.1 dynamic_slice.7.scale_ref
  19.1 30.6 %all-to-all-done = bf16[16,2,40,256]{3,2,1,0:T(8,128)(2,1)S(1)} async-done(((bf16[16,2,40,256]{3,2,1,0:T(8,128)(2,1)}), bf16[16,2,40,256]{3,2,1,0:T(8,128)(2,1)S(1)}, u32[]{:S(2)}, u32[]{:S(2)}) %all-to-all-start) | async-done | bytes 655392 | tf_op jit(solution)/shard_map/cond/branch_1_fun/all_to_all | solution.py:136
  49.7 0.1 pad.3.clone
  49.8 11.8 %branch_1_fun.1 = bf16[2,768,256]{2,1,0:T(8,128)(2,1)S(1)} custom-call(f32[2]{0:T(128)S(1)} %dynamic_slice.6.width_ref, f32[2]{0:T(128)S(1)} %dynamic_slice.7.scale_ref, bf16[2,768,256]{2,1,0:T(8,128)(2,1)S(1)} %bitcast.17), custom_call_target="tpu_custom_call" | custom-call | tf_op jit(solution)/shard_map/cond/branch_1_fun/pallas_call | solution.py:107
  61.6 58.9 %all_to_all.8 = bf16[16,2,40,256]{3,2,1,0:T(8,128)(2,1)} all-to-all(bf16[16,2,40,256]{3,2,1,0:T(8,128)(2,1)S(1)} %copy_bitcast_fusion), channel_id=1, replica_groups=mesh['lat'=32,'lon'=16] {'lon'}, dimensions={0} | all-to-all | bytes 1310720 | tf_op jit(solution)/shard_map/cond/branch_1_fun/all_to_all | solution.py:147
  120.5 1.2 fusion.38
  121.7 0.1 copy.30
  121.8 0.1 copy.32
  122.0 1.3 collective-permute-start.3
  123.3 1.3 collective-permute-start.4
  124.6 0.1 broadcast_select_fusion.1
  124.6 0.7 collective-permute-start.2
  125.4 0.2 select_reduce_fusion
  125.6 1.2 copy.28
  126.8 0.0 collective-permute-done.2
  126.8 7.2 %collective-permute-done.3 = bf16[24,40,256]{2,0,1:T(8,128)(2,1)S(1)} collective-permute-done((bf16[24,40,256]{2,0,1:T(8,128)(2,1)S(1)}, bf16[24,40,256]{2,0,1:T(8,128)(2,1)S(1)}, u32[]{:S(2)}, u32[]{:S(2)}) %collective-permute-start.3) | collective-permute-done | bytes 491552 | tf_op jit(solution)/shard_map/ppermute | solution.py:165
  134.0 3.8 %collective-permute-done.4 = bf16[24,40,256]{2,0,1:T(8,128)(2,1)S(1)} collective-permute-done((bf16[24,40,256]{2,0,1:T(8,128)(2,1)S(1)}, bf16[24,40,256]{2,0,1:T(8,128)(2,1)S(1)}, u32[]{:S(2)}, u32[]{:S(2)}) %collective-permute-start.4) | collective-permute-done | bytes 491552 | tf_op jit(solution)/shard_map/ppermute | solution.py:168
  137.8 0.1 broadcast_select_fusion.2
  137.9 1.4 %fusion.9 = f32[40,32,256]{2,1,0:T(8,128)} fusion(bf16[24,40,256]{2,0,1:T(8,128)(2,1)S(1)} %get-tuple-element.47, bf16[32,40,256]{2,0,1:T(8,128)(2,1)S(1)} %copy.28, bf16[24,40,256]{2,0,1:T(8,128)(2,1)S(1)} %get-tuple-element.46, f32[32]{0:T(128)S(1)} %sqrt.7, s32[80]{0:T(128)S(1)} %iota_add_fusion.2), kind=kOutput, calls=%fused_computation.8 | convolution fusion | flops 57694720 | bytes 2949568 | tf_op jit(solution)/shard_map/jmc,jr->mrc/dot_general | solution.py:221
  (10 shorter events, 0.1 us)
Async XLA Ops:
  2.3 2.5 %collective-permute-start = (bf16[32,40,256]{2,1,0:T(8,128)(2,1)}, bf16[32,40,256]{2,1,0:T(8,128)(2,1)S(1)}, u32[]{:S(2)}, u32[]{:S(2)}) collective-permute-start(bf16[32,40,256]{2,1,0:T(8,128)(2,1)} %bitcast.16), channel_id=1, source_target_pairs={{32,33},{33,34},{34,35},{35,36},{36,37},{37,38},{38,39},{39,40},{4... | collective-permute-start | bytes 1966088 | tf_op jit(solution)/shard_map/ppermute | solution.py:188
  3.0 1.9 %collective-permute-start.1 = (bf16[32,40,256]{2,1,0:T(8,128)(2,1)}, bf16[32,40,256]{2,1,0:T(8,128)(2,1)S(1)}, u32[]{:S(2)}, u32[]{:S(2)}) collective-permute-start(bf16[32,40,256]{2,1,0:T(8,128)(2,1)} %bitcast.16), channel_id=1, source_target_pairs={{32,47},{33,32},{34,33},{35,34},{36,35},{37,36},{38,37},{39,38},{4... | collective-permute-start | bytes 1966088 | tf_op jit(solution)/shard_map/ppermute | solution.py:191
  4.9 44.8 %all-to-all-start = ((bf16[16,2,40,256]{3,2,1,0:T(8,128)(2,1)}), bf16[16,2,40,256]{3,2,1,0:T(8,128)(2,1)S(1)}, u32[]{:S(2)}, u32[]{:S(2)}) async-start(bf16[16,2,40,256]{3,2,1,0:T(8,128)(2,1)} %bitcast), calls=%async_computation | async-start | bytes 1310720 | tf_op jit(solution)/shard_map/cond/branch_1_fun/all_to_all | solution.py:136
  122.0 12.0 %collective-permute-start.3 = (bf16[24,40,256]{2,0,1:T(8,128)(2,1)S(1)}, bf16[24,40,256]{2,0,1:T(8,128)(2,1)S(1)}, u32[]{:S(2)}, u32[]{:S(2)}) collective-permute-start(bf16[24,40,256]{2,0,1:T(8,128)(2,1)S(1)} %get-tuple-element.38), channel_id=1, source_target_pairs={{0,16},{1,17},{2,18},{3,19},{4,20},{5,21},{6,22},{7,23},{8,24},{9,... | collective-permute-start | bytes 1474568 | tf_op jit(solution)/shard_map/ppermute | solution.py:165
  123.3 14.5 %collective-permute-start.4 = (bf16[24,40,256]{2,0,1:T(8,128)(2,1)S(1)}, bf16[24,40,256]{2,0,1:T(8,128)(2,1)S(1)}, u32[]{:S(2)}, u32[]{:S(2)}) collective-permute-start(bf16[24,40,256]{2,0,1:T(8,128)(2,1)S(1)} %get-tuple-element.39), channel_id=1, source_target_pairs={{16,0},{17,1},{18,2},{19,3},{20,4},{21,5},{22,6},{23,7},{24,8},{25... | collective-permute-start | bytes 1474568 | tf_op jit(solution)/shard_map/ppermute | solution.py:168
  124.6 2.2 %collective-permute-start.2 = (bf16[24,40,256]{2,0,1:T(8,128)(2,1)S(1)}, bf16[24,40,256]{2,0,1:T(8,128)(2,1)S(1)}, u32[]{:S(2)}, u32[]{:S(2)}) collective-permute-start(bf16[24,40,256]{2,0,1:T(8,128)(2,1)S(1)} %broadcast_select_fusion.1), channel_id=1, source_target_pairs={{48,64},{49,65},{50,66},{51,67},{52,68},{53,69},{54,70},{55,71},{5... | collective-permute-start | bytes 1474568 | tf_op jit(solution)/shard_map/ppermute | solution.py:156

commit v2 on v1

--- a/solution.py
+++ b/solution.py
@@ -10,6 +10,7 @@
 HALF_LAT = 24
 POLAR = 64
 X_RUN = 4
+HELPERS = {0: (10, 26, 17, 18), 1: (1, 9, 25, 2), 30: (30, 22, 6, 29), 31: (21, 5, 14, 13)}
 TILE = 128
 
 
@@ -96,7 +97,7 @@
             total[...] += jnp.dot(data, weights, preferred_element_type=jnp.float32)
             return carry
 
-        lax.fori_loop(0, blocks, step, 0)
+        lax.fori_loop(0, blocks, step, 0, unroll=4)
         out_ref[row] = total[...].astype(jnp.bfloat16)
 
 
@@ -127,48 +128,39 @@
     return 1.0 / jnp.sqrt(jnp.sum(weights_raw * weights_raw, axis=1))
 
 
-def polar_along(data, widths, scales):
-    rows, members, cols = data.shape
-    lon_count = lax.axis_size("lon")
-    own = rows // lon_count
-    padded = -members % 16
-    parts = data.reshape(lon_count, own, members, cols)
-    parts = lax.all_to_all(parts, "lon", 0, 0)
-    parts = jnp.pad(parts.transpose(1, 0, 2, 3), ((0, 0), (0, 0), (0, padded), (0, 0)))
-    parts = parts.reshape(own, lon_count * (members + padded), cols)
-    first = lax.axis_index("lon") * own
-    result = circle_product(
-        parts,
-        lax.dynamic_slice_in_dim(widths, first, own),
-        lax.dynamic_slice_in_dim(scales, first, own),
-        lon_count,
-    )
-    result = result.reshape(own, lon_count, members + padded, cols)[:, :, :members]
-    result = lax.all_to_all(result.transpose(1, 0, 2, 3), "lon", 0, 0)
-    return result.reshape(rows, members, cols)
-
-
-def lat_halo(along, lat_index, lat_count, lon_count):
+def unit_product(parts, width, scale):
+    blocks, members, cols = parts.shape
+    padded = members + -members % 16
+    data = jnp.pad(parts, ((0, 0), (0, padded - members), (0, 0)))
+    result = circle_product(data.reshape(1, blocks * padded, cols), width, scale, blocks)
+    return result.reshape(blocks, padded, cols)[:, :members]
+
+
+def far_halo(near, lat_index, lat_count, lon_count):
+    last = X_RUN - 1
+    send = jnp.where(lat_index % X_RUN == last, near[-HALF_LAT:], near[:HALF_LAT])
+
+    def across(lat, lon):
+        return {last: (lat + 1, lon), 0: (lat - 1, lon)}.get(lat % X_RUN)
+
+    return lax.ppermute(send, ("lat", "lon"), flat_pairs(lat_count, lon_count, across))
+
+
+def next_halo(along, lat_count, lon_count):
     axes = ("lat", "lon")
-    last, x = X_RUN - 1, lat_index % X_RUN
+    last = X_RUN - 1
     pairs = functools.partial(flat_pairs, lat_count, lon_count)
-    lower, upper = along[:HALF_LAT], along[-HALF_LAT:]
-    far = lax.ppermute(
-        jnp.where(x == last, upper, lower),
+    low = lax.ppermute(
+        along[-HALF_LAT:],
         axes,
-        pairs(
-            lambda lat, lon: (lat + 1, lon)
-            if lat % X_RUN == last
-            else ((lat - 1, lon) if lat % X_RUN == 0 else None)
-        ),
-    )
-    low = lax.ppermute(
-        upper, axes, pairs(lambda lat, lon: (lat + 1, lon) if lat % X_RUN != last else None)
+        pairs(lambda lat, lon: (lat + 1, lon) if lat % X_RUN != last else None),
     )
     high = lax.ppermute(
-        lower, axes, pairs(lambda lat, lon: (lat - 1, lon) if lat % X_RUN != 0 else None)
-    )
-    return jnp.where(x == 0, far, low), jnp.where(x == last, far, high)
+        along[:HALF_LAT],
+        axes,
+        pairs(lambda lat, lon: (lat - 1, lon) if lat % X_RUN != 0 else None),
+    )
+    return low, high
 
 
 def body(members, support):
@@ -185,6 +177,35 @@
 
     pairs = functools.partial(flat_pairs, lat_count, lon_count)
     data = members.transpose(1, 0, 2)
+    lon_index = lax.axis_index("lon")
+
+    shares = len(HELPERS[0])
+    share = lat_rows // shares
+    helped = {h: (p, q) for p, hs in HELPERS.items() for q, h in enumerate(hs)}
+    pieces = lon_count // share
+    is_polar = polar_of(lat_index)
+    takes_part = functools.reduce(lambda a, b: a | b, [lat_index == i for i in helped])
+    keeps = functools.reduce(lambda a, b: a | b, [lat_index == p for p in HELPERS if p in helped])
+    row_of = jnp.array(
+        [helped[i][0] * lat_rows + helped[i][1] * share if i in helped else 0 for i in range(lat_count)]
+    )[lat_index]
+
+    def hands(q):
+        return lambda lat, lon: (
+            (HELPERS[lat][q], lon) if lat in HELPERS and HELPERS[lat][q] != lat else None
+        )
+
+    def returns(q):
+        return lambda lat, lon: (
+            (helped[lat][0], lon) if lat in helped and helped[lat][1] == q and helped[lat][0] != lat else None
+        )
+
+    handed = [
+        lax.ppermute(data[q * share : (q + 1) * share], axes, pairs(hands(q))) for q in range(shares)
+    ]
+    given = jnp.where(keeps, data[:share], sum(handed))
+    parts = given.reshape(lon_count, member_count // pieces, lon_cols)
+
     left = lax.ppermute(
         data, axes, pairs(lambda lat, lon: None if polar_of(lat) else (lat, lon + 1))
     )
@@ -192,15 +213,25 @@
         data, axes, pairs(lambda lat, lon: None if polar_of(lat) else (lat, lon - 1))
     )
     widths = lax.dynamic_slice_in_dim(support, lat_index * lat_rows, lat_rows).astype(jnp.float32)
-    scales = row_scale(widths, nlon_all)
-    along = lax.cond(
-        polar_of(lat_index),
-        lambda: polar_along(data, widths, scales),
-        lambda: near_product(left, data, right, widths, scales),
-    )
-
-    low, high = lat_halo(along, lat_index, lat_count, lon_count)
-    widened = jnp.concatenate([low, along, high], axis=0)
+    unit_width = lax.dynamic_slice_in_dim(support, row_of + lon_index // pieces, 1).astype(jnp.float32)
+    scales = row_scale(jnp.concatenate([widths, unit_width]), nlon_all)
+    scales, unit_scale = scales[:lat_rows], scales[lat_rows:]
+
+    def helping(parts):
+        parts = lax.all_to_all(parts, "lon", 0, 0)
+        return lax.all_to_all(unit_product(parts, unit_width, unit_scale), "lon", 0, 0)
+
+    parts = lax.cond(takes_part, helping, lambda v: v, parts)
+    parts, left, right = lax.optimization_barrier((parts, left, right))
+    near = near_product(left, data, right, widths, scales)
+
+    far = far_halo(near, lat_index, lat_count, lon_count)
+    done = parts.reshape(share, member_count, lon_cols)
+    polar = [lax.ppermute(done, axes, pairs(returns(q))) for q in range(shares)]
+    polar[0] = jnp.where(keeps, done, polar[0])
+    polar = jnp.concatenate(polar, axis=0)
+    along = jnp.where(is_polar, polar, near)
+    low, high = next_halo(along, lat_count, lon_count)
 
     half_rows = HALF_LAT
     source_rows = jnp.arange(lat_rows + 2 * half_rows)
@@ -218,8 +249,23 @@
     reached = global_rows[:, None] + offsets[None, :]
     inside = (reached >= 0) & (reached < nlat_all)
     lat_norms = 1.0 / jnp.sqrt(jnp.sum(jnp.where(inside, (values * values)[None, :], 0.0), axis=1))
-    smoothed = jnp.einsum("jmc,jr->mrc", widened, banded, preferred_element_type=jnp.float32)
-    return smoothed * lat_norms[None, :, None]
+    lower, own, upper = banded[:half_rows], banded[half_rows:-half_rows], banded[-half_rows:]
+    x = lat_index % X_RUN
+    taps = jnp.where(x == 0, lower, upper)
+    first = jnp.einsum(
+        "jmc,jr->mrc",
+        jnp.concatenate([far, along], axis=0),
+        jnp.concatenate([taps, own], axis=0),
+        preferred_element_type=jnp.float32,
+    )
+    first = lax.optimization_barrier(first)
+    second = jnp.einsum(
+        "jmc,jr->mrc",
+        jnp.concatenate([low, high], axis=0),
+        jnp.concatenate([lower, upper], axis=0),
+        preferred_element_type=jnp.float32,
+    )
+    return (first + second) * lat_norms[None, :, None]
 
 
 def solution(mesh):

time: 140 us -> 111 us (0.79)
  blocking collectives: 58.9 us -> 0 us
  waiting for transfers between devices: 41.6 us -> 69.7 us
  Pallas kernels: 11.8 us -> 4.03 us
  starting transfers between devices: 18.8 us -> 26.3 us
  between operations: 0.17 us -> 1.66 us
    all_to_all x1 -> x0, blocking collectives: 58.9 us -> none  [polar_along(): result = lax.all_to_all(result.transpose(1, 0, 2, 3), 'lon', 0, 0)]
    ppermute x3 -> x11, waiting for transfers between devices: 11 us -> 69.7 us  [the longest x4 54 us: body(): polar = [lax.ppermute(done, axes, pairs(returns(q))) for q in range(shares)]]
    all_to_all x1 -> x0, waiting for transfers between devices: 30.6 us -> none  [polar_along(): parts = lax.all_to_all(parts, 'lon', 0, 0)]
    ppermute x3 -> x11, starting transfers between devices: 3.3 us -> 24.9 us  [the longest x4 16.5 us: body(): lax.ppermute(data[q * share:(q + 1) * share], axes, pairs(hands(q)))]
    all_to_all x1 -> x0, starting transfers between devices: 14.1 us -> none  [polar_along(): parts = lax.all_to_all(parts, 'lon', 0, 0)]
    pallas_call x1, Pallas kernels: 11.8 us -> 4.03 us  [near_product(): pl.pallas_call(near_kernel, grid=(rows // step,), in_specs=[smem, smem, b...]
    dynamic_slice x2, local copies, waits for them, and re-layouts: 0.15 us -> 1.86 us  [the longest x1 1.27 us: body(): lax.dynamic_slice_in_dim(support, row_of + lon_index // pieces, 1)]
    reshape x0 -> x2, local copies, waits for them, and re-layouts: none -> 1.68 us  [the longest x1 0.97 us: body(): done = parts.reshape(share, member_count, lon_cols)]
  transfers between devices with their start and end apart: 6 -> 13, of which waited for: 3 -> 4; matrix products, arithmetic and copies ran while one was open for 2% -> 5% of each run, Pallas kernels for 0% -> 4%
where the time goes in v2:
time: 111 us
  waiting for transfers between devices  69.7 us (63%)
  starting transfers between devices  26.3 us (24%)
  local copies, waits for them, and re-layouts  5.2 us (5%)
  Pallas kernels  4.03 us (4%)
  other arithmetic  1.92 us (2%)
  matrix products  1.88 us (2%)
  between operations  1.66 us (1%)
    ppermute x4, waiting for transfers between devices, body(): polar = [lax.ppermute(done, axes, pairs(returns(q))) for q in range(shares)]  54 us
    ppermute x4, starting transfers between devices, body(): lax.ppermute(data[q * share:(q + 1) * share], axes, pairs(hands(q)))  16.5 us
    ppermute x1, waiting for transfers between devices, next_halo(): lax.ppermute(along[-HALF_LAT:], axes, pairs(lambda lat, lon: (lat + 1, lo...  8.95 us
    ppermute x4, starting transfers between devices, body(): polar = [lax.ppermute(done, axes, pairs(returns(q))) for q in range(shares)]  5.17 us
    pallas_call x1, Pallas kernels, near_product(): pl.pallas_call(near_kernel, grid=(rows // step,), in_specs=[smem, smem, b...  4.03 us
    ppermute x1, waiting for transfers between devices, next_halo(): lax.ppermute(along[:HALF_LAT], axes, pairs(lambda lat, lon: (lat - 1, lon...  3.94 us
    ppermute x4, waiting for transfers between devices, body(): lax.ppermute(data[q * share:(q + 1) * share], axes, pairs(hands(q)))  2.75 us
  transfers between devices with their start and end apart: 13, of which 4 were waited for; matrix products, arithmetic and copies ran while one was open for 5% of the time, Pallas kernels for 4%

profile of v2, /device:TPU:1, one launch (start us, length us, event | category | flops | bytes accessed | tf_op | source)
XLA Modules:
  0.0 110.7 jit_solution(10765763490062394168)
XLA Ops:
  0.0 1.5 %copy.18 = bf16[40,32,256]{2,0,1:T(8,128)(2,1)S(1)} copy(bf16[40,32,256]{2,1,0:T(8,128)(2,1)} %param.5) | data formatting | bytes 1310720 | tf_op args[0]
  1.5 0.7 collective-permute-start.4
  2.2 0.7 collective-permute-start.5
  2.9 12.6 %collective-permute-start.1 = (bf16[8,40,256]{2,1,0:T(8,128)(2,1)S(1)}, bf16[8,40,256]{2,1,0:T(8,128)(2,1)S(1)}, u32[]{:S(2)}, u32[]{:S(2)}) collective-permute-start(bf16[8,40,256]{2,1,0:T(8,128)(2,1)S(1)} %get-tuple-element.29), channel_id=1, source_target_pairs={{0,416},{1,417},{2,418},{3,419},{4,420},{5,421},{6,422},{7,423},{8... | collective-permute-start | bytes 491528 | tf_op jit(solution)/shard_map/ppermute | solution.py:204
  15.5 1.3 %collective-permute-start.3 = (bf16[8,40,256]{2,1,0:T(8,128)(2,1)S(1)}, bf16[8,40,256]{2,1,0:T(8,128)(2,1)S(1)}, u32[]{:S(2)}, u32[]{:S(2)}) collective-permute-start(bf16[8,40,256]{2,1,0:T(8,128)(2,1)S(1)} %get-tuple-element.30), channel_id=1, source_target_pairs={{0,288},{1,289},{2,290},{3,291},{4,292},{5,293},{6,294},{7,295},{8... | collective-permute-start | bytes 491528 | tf_op jit(solution)/shard_map/ppermute | solution.py:204
  16.8 1.3 %collective-permute-start.2 = (bf16[8,40,256]{2,1,0:T(8,128)(2,1)S(1)}, bf16[8,40,256]{2,1,0:T(8,128)(2,1)S(1)}, u32[]{:S(2)}, u32[]{:S(2)}) collective-permute-start(bf16[8,40,256]{2,1,0:T(8,128)(2,1)S(1)} %get-tuple-element.31), channel_id=1, source_target_pairs={{0,272},{1,273},{2,274},{3,275},{4,276},{5,277},{6,278},{7,279},{8... | collective-permute-start | bytes 491528 | tf_op jit(solution)/shard_map/ppermute | solution.py:204
  18.2 0.6 dynamic_slice.10
  19.5 0.8 dynamic-slice_convert_fusion.width_ref
  20.2 1.3 %dynamic_slice.11 = s32[1]{0:T(128)} dynamic-slice(s32[1024]{0:T(1024)} %param.6, s32[]{:T(128)S(6)} %select_n.86), dynamic_slice_sizes={1} | dynamic-slice | bytes 12 | tf_op jit(solution)/shard_map/dynamic_slice | solution.py:216
  22.2 0.1 fusion.22
  22.3 0.3 fusion.6
  22.7 1.3 %collective-permute-start = (bf16[8,40,256]{2,1,0:T(8,128)(2,1)S(1)}, bf16[8,40,256]{2,1,0:T(8,128)(2,1)S(1)}, u32[]{:S(2)}, u32[]{:S(2)}) collective-permute-start(bf16[8,40,256]{2,1,0:T(8,128)(2,1)S(1)} %get-tuple-element.32), channel_id=1, source_target_pairs={{0,160},{1,161},{2,162},{3,163},{4,164},{5,165},{6,166},{7,167},{8... | collective-permute-start | bytes 491528 | tf_op jit(solution)/shard_map/ppermute | solution.py:204
  24.1 2.7 %collective-permute-done = bf16[8,40,256]{2,1,0:T(8,128)(2,1)S(1)} collective-permute-done((bf16[8,40,256]{2,1,0:T(8,128)(2,1)S(1)}, bf16[8,40,256]{2,1,0:T(8,128)(2,1)S(1)}, u32[]{:S(2)}, u32[]{:S(2)}) %collective-permute-start) | collective-permute-done | bytes 163872 | tf_op jit(solution)/shard_map/ppermute | solution.py:204
  26.9 0.7 reshape.69
  27.6 1.0 reshape.70
  28.6 1.3 %collective-permute-start.10 = (bf16[8,40,256]{2,1,0:T(8,128)(2,1)S(1)}, bf16[8,40,256]{2,1,0:T(8,128)(2,1)S(1)}, u32[]{:S(2)}, u32[]{:S(2)}) collective-permute-start(bf16[8,40,256]{2,1,0:T(8,128)(2,1)S(1)} %reshape.70), channel_id=1, source_target_pairs={{32,16},{33,17},{34,18},{35,19},{36,20},{37,21},{38,22},{39,23},{4... | collective-permute-start | bytes 491528 | tf_op jit(solution)/shard_map/ppermute | solution.py:230
  29.9 1.3 %collective-permute-start.9 = (bf16[8,40,256]{2,1,0:T(8,128)(2,1)S(1)}, bf16[8,40,256]{2,1,0:T(8,128)(2,1)S(1)}, u32[]{:S(2)}, u32[]{:S(2)}) collective-permute-start(bf16[8,40,256]{2,1,0:T(8,128)(2,1)S(1)} %reshape.70), channel_id=1, source_target_pairs={{96,480},{97,481},{98,482},{99,483},{100,484},{101,485},{102,486},... | collective-permute-start | bytes 491528 | tf_op jit(solution)/shard_map/ppermute | solution.py:230
  31.2 1.3 %collective-permute-start.8 = (bf16[8,40,256]{2,1,0:T(8,128)(2,1)S(1)}, bf16[8,40,256]{2,1,0:T(8,128)(2,1)S(1)}, u32[]{:S(2)}, u32[]{:S(2)}) collective-permute-start(bf16[8,40,256]{2,1,0:T(8,128)(2,1)S(1)} %reshape.70), channel_id=1, source_target_pairs={{80,496},{81,497},{82,498},{83,499},{84,500},{85,501},{86,502},{87... | collective-permute-start | bytes 491528 | tf_op jit(solution)/shard_map/ppermute | solution.py:230
  32.5 1.3 %collective-permute-start.7 = (bf16[8,40,256]{2,1,0:T(8,128)(2,1)S(1)}, bf16[8,40,256]{2,1,0:T(8,128)(2,1)S(1)}, u32[]{:S(2)}, u32[]{:S(2)}) collective-permute-start(bf16[8,40,256]{2,1,0:T(8,128)(2,1)S(1)} %reshape.70), channel_id=1, source_target_pairs={{160,0},{161,1},{162,2},{163,3},{164,4},{165,5},{166,6},{167,7},{1... | collective-permute-start | bytes 491528 | tf_op jit(solution)/shard_map/ppermute | solution.py:230
  33.8 4.0 %shard_map.37 = bf16[32,40,256]{2,1,0:T(8,128)(2,1)S(1)} custom-call(f32[32]{0:T(128)S(1)} %dynamic-slice_convert_fusion.width_ref, f32[32]{0:T(128)S(1)} %bitcast.28, bf16[32,40,256]{2,1,0:T(8,128)(2,1)S(1)} %collective-permute-done.4.left_ref, bf16[32,40,256]{2,1,0:T(8,128)(2,1)S(1)} %bitcast.25, bf16[32,40,256]{2,1,0:T(8,128)(2,1)S(1)} %collective-permute-done.5.right_ref), custom_call_target="tpu_custom_call" | custom-call | tf_op jit(solution)/shard_map/pallas_call | solution.py:66
  37.9 0.7 collective-permute-start.6
  38.6 54.0 %collective-permute-done.7 = bf16[8,40,256]{2,1,0:T(8,128)(2,1)S(1)} collective-permute-done((bf16[8,40,256]{2,1,0:T(8,128)(2,1)S(1)}, bf16[8,40,256]{2,1,0:T(8,128)(2,1)S(1)}, u32[]{:S(2)}, u32[]{:S(2)}) %collective-permute-start.7) | collective-permute-done | bytes 163872 | tf_op jit(solution)/shard_map/ppermute | solution.py:230
  92.7 0.1 maximum_select_fusion
  92.9 1.3 %collective-permute-start.11 = (bf16[24,40,256]{2,1,0:T(8,128)(2,1)S(1)}, bf16[24,40,256]{2,1,0:T(8,128)(2,1)S(1)}, u32[]{:S(2)}, u32[]{:S(2)}) collective-permute-start(bf16[24,40,256]{2,1,0:T(8,128)(2,1)S(1)} %get-tuple-element.27), channel_id=1, source_target_pairs={{0,16},{1,17},{2,18},{3,19},{4,20},{5,21},{6,22},{7,23},{8,24},{9,... | collective-permute-start | bytes 1474568 | tf_op jit(solution)/shard_map/ppermute | solution.py:153
  94.2 1.3 %collective-permute-start.12 = (bf16[24,40,256]{2,1,0:T(8,128)(2,1)S(1)}, bf16[24,40,256]{2,1,0:T(8,128)(2,1)S(1)}, u32[]{:S(2)}, u32[]{:S(2)}) collective-permute-start(bf16[24,40,256]{2,1,0:T(8,128)(2,1)S(1)} %get-tuple-element.28), channel_id=1, source_target_pairs={{16,0},{17,1},{18,2},{19,3},{20,4},{21,5},{22,6},{23,7},{24,8},{25... | collective-permute-start | bytes 1474568 | tf_op jit(solution)/shard_map/ppermute | solution.py:158
  95.5 0.2 select_reduce_fusion
  95.7 0.1 pad_maximum_fusion
  95.8 0.4 convolution_bitcast_fusion.1
  96.3 8.9 %collective-permute-done.11 = bf16[24,40,256]{2,1,0:T(8,128)(2,1)S(1)} collective-permute-done((bf16[24,40,256]{2,1,0:T(8,128)(2,1)S(1)}, bf16[24,40,256]{2,1,0:T(8,128)(2,1)S(1)}, u32[]{:S(2)}, u32[]{:S(2)}) %collective-permute-start.11) | collective-permute-done | bytes 491552 | tf_op jit(solution)/shard_map/ppermute | solution.py:153
  105.2 3.9 %collective-permute-done.12 = bf16[24,40,256]{2,1,0:T(8,128)(2,1)S(1)} collective-permute-done((bf16[24,40,256]{2,1,0:T(8,128)(2,1)S(1)}, bf16[24,40,256]{2,1,0:T(8,128)(2,1)S(1)}, u32[]{:S(2)}, u32[]{:S(2)}) %collective-permute-start.12) | collective-permute-done | bytes 491552 | tf_op jit(solution)/shard_map/ppermute | solution.py:158
  109.1 0.1 pad_maximum_fusion.1
  109.2 1.5 %fusion.1 = f32[40,32,256]{2,1,0:T(8,128)} fusion(f32[40,32,256]{2,1,0:T(8,128)S(1)} %convolution_bitcast_fusion.1, bf16[48,40,256]{2,1,0:T(8,128)(2,1)S(1)} %pad_maximum_fusion.1, f32[32]{0:T(128)S(1)} %sqrt.7, bf16[24,32]{0,1:T(8,128)(2,1)S(1)} %get-tuple-element.35, bf16[24,32]{0,1:T(8,128)(2,1)S(1)} %get-tuple-element.33), kind=kOutput, calls=%fused_computation.2 | convolution fusion | flops 32118784 | bytes 3607680 | tf_op jit(solution)/shard_map/jmc,jr->mrc/dot_general | solution.py:262
  (28 shorter events, 0.5 us)
Async XLA Ops:
  0.0 18.2 %copy-start = (s32[32]{0:T(128)S(1)}, s32[32]{0:T(128)}, u32[]{:S(2)}) copy-start(s32[32]{0:T(128)} %constant.105.clone) | copy-start | bytes 388
  1.5 26.2 %collective-permute-start.4 = (bf16[32,40,256]{2,1,0:T(8,128)(2,1)S(1)}, bf16[32,40,256]{2,1,0:T(8,128)(2,1)S(1)}, u32[]{:S(2)}, u32[]{:S(2)}) collective-permute-start(bf16[32,40,256]{2,1,0:T(8,128)(2,1)S(1)} %bitcast.21), channel_id=1, source_target_pairs={{32,33},{33,34},{34,35},{35,36},{36,37},{37,38},{38,39},{39,40},{4... | collective-permute-start | bytes 1966088 | tf_op jit(solution)/shard_map/ppermute | solution.py:209
  2.2 25.5 %collective-permute-start.5 = (bf16[32,40,256]{2,1,0:T(8,128)(2,1)S(1)}, bf16[32,40,256]{2,1,0:T(8,128)(2,1)S(1)}, u32[]{:S(2)}, u32[]{:S(2)}) collective-permute-start(bf16[32,40,256]{2,1,0:T(8,128)(2,1)S(1)} %bitcast.22), channel_id=1, source_target_pairs={{32,47},{33,32},{34,33},{35,34},{36,35},{37,36},{38,37},{39,38},{4... | collective-permute-start | bytes 1966088 | tf_op jit(solution)/shard_map/ppermute | solution.py:212
  2.9 19.7 %collective-permute-start.1 = (bf16[8,40,256]{2,1,0:T(8,128)(2,1)S(1)}, bf16[8,40,256]{2,1,0:T(8,128)(2,1)S(1)}, u32[]{:S(2)}, u32[]{:S(2)}) collective-permute-start(bf16[8,40,256]{2,1,0:T(8,128)(2,1)S(1)} %get-tuple-element.29), channel_id=1, source_target_pairs={{0,416},{1,417},{2,418},{3,419},{4,420},{5,421},{6,422},{7,423},{8... | collective-permute-start | bytes 491528 | tf_op jit(solution)/shard_map/ppermute | solution.py:204
  15.5 8.6 %collective-permute-start.3 = (bf16[8,40,256]{2,1,0:T(8,128)(2,1)S(1)}, bf16[8,40,256]{2,1,0:T(8,128)(2,1)S(1)}, u32[]{:S(2)}, u32[]{:S(2)}) collective-permute-start(bf16[8,40,256]{2,1,0:T(8,128)(2,1)S(1)} %get-tuple-element.30), channel_id=1, source_target_pairs={{0,288},{1,289},{2,290},{3,291},{4,292},{5,293},{6,294},{7,295},{8... | collective-permute-start | bytes 491528 | tf_op jit(solution)/shard_map/ppermute | solution.py:204
  16.8 7.3 %collective-permute-start.2 = (bf16[8,40,256]{2,1,0:T(8,128)(2,1)S(1)}, bf16[8,40,256]{2,1,0:T(8,128)(2,1)S(1)}, u32[]{:S(2)}, u32[]{:S(2)}) collective-permute-start(bf16[8,40,256]{2,1,0:T(8,128)(2,1)S(1)} %get-tuple-element.31), channel_id=1, source_target_pairs={{0,272},{1,273},{2,274},{3,275},{4,276},{5,277},{6,278},{7,279},{8... | collective-permute-start | bytes 491528 | tf_op jit(solution)/shard_map/ppermute | solution.py:204
  22.7 4.2 %collective-permute-start = (bf16[8,40,256]{2,1,0:T(8,128)(2,1)S(1)}, bf16[8,40,256]{2,1,0:T(8,128)(2,1)S(1)}, u32[]{:S(2)}, u32[]{:S(2)}) collective-permute-start(bf16[8,40,256]{2,1,0:T(8,128)(2,1)S(1)} %get-tuple-element.32), channel_id=1, source_target_pairs={{0,160},{1,161},{2,162},{3,163},{4,164},{5,165},{6,166},{7,167},{8... | collective-permute-start | bytes 491528 | tf_op jit(solution)/shard_map/ppermute | solution.py:204
  28.6 64.0 %collective-permute-start.10 = (bf16[8,40,256]{2,1,0:T(8,128)(2,1)S(1)}, bf16[8,40,256]{2,1,0:T(8,128)(2,1)S(1)}, u32[]{:S(2)}, u32[]{:S(2)}) collective-permute-start(bf16[8,40,256]{2,1,0:T(8,128)(2,1)S(1)} %reshape.70), channel_id=1, source_target_pairs={{32,16},{33,17},{34,18},{35,19},{36,20},{37,21},{38,22},{39,23},{4... | collective-permute-start | bytes 491528 | tf_op jit(solution)/shard_map/ppermute | solution.py:230
  29.9 62.7 %collective-permute-start.9 = (bf16[8,40,256]{2,1,0:T(8,128)(2,1)S(1)}, bf16[8,40,256]{2,1,0:T(8,128)(2,1)S(1)}, u32[]{:S(2)}, u32[]{:S(2)}) collective-permute-start(bf16[8,40,256]{2,1,0:T(8,128)(2,1)S(1)} %reshape.70), channel_id=1, source_target_pairs={{96,480},{97,481},{98,482},{99,483},{100,484},{101,485},{102,486},... | collective-permute-start | bytes 491528 | tf_op jit(solution)/shard_map/ppermute | solution.py:230
  31.2 61.4 %collective-permute-start.8 = (bf16[8,40,256]{2,1,0:T(8,128)(2,1)S(1)}, bf16[8,40,256]{2,1,0:T(8,128)(2,1)S(1)}, u32[]{:S(2)}, u32[]{:S(2)}) collective-permute-start(bf16[8,40,256]{2,1,0:T(8,128)(2,1)S(1)} %reshape.70), channel_id=1, source_target_pairs={{80,496},{81,497},{82,498},{83,499},{84,500},{85,501},{86,502},{87... | collective-permute-start | bytes 491528 | tf_op jit(solution)/shard_map/ppermute | solution.py:230
  32.5 60.1 %collective-permute-start.7 = (bf16[8,40,256]{2,1,0:T(8,128)(2,1)S(1)}, bf16[8,40,256]{2,1,0:T(8,128)(2,1)S(1)}, u32[]{:S(2)}, u32[]{:S(2)}) collective-permute-start(bf16[8,40,256]{2,1,0:T(8,128)(2,1)S(1)} %reshape.70), channel_id=1, source_target_pairs={{160,0},{161,1},{162,2},{163,3},{164,4},{165,5},{166,6},{167,7},{1... | collective-permute-start | bytes 491528 | tf_op jit(solution)/shard_map/ppermute | solution.py:230
  37.9 57.8 %collective-permute-start.6 = (bf16[24,40,256]{2,1,0:T(8,128)(2,1)S(1)}, bf16[24,40,256]{2,1,0:T(8,128)(2,1)S(1)}, u32[]{:S(2)}, u32[]{:S(2)}) collective-permute-start(bf16[24,40,256]{2,1,0:T(8,128)(2,1)S(1)} %slice_select_fusion), channel_id=1, source_target_pairs={{48,64},{49,65},{50,66},{51,67},{52,68},{53,69},{54,70},{55,71},{5... | collective-permute-start | bytes 1474568 | tf_op jit(solution)/shard_map/ppermute | solution.py:146
  92.9 12.3 %collective-permute-start.11 = (bf16[24,40,256]{2,1,0:T(8,128)(2,1)S(1)}, bf16[24,40,256]{2,1,0:T(8,128)(2,1)S(1)}, u32[]{:S(2)}, u32[]{:S(2)}) collective-permute-start(bf16[24,40,256]{2,1,0:T(8,128)(2,1)S(1)} %get-tuple-element.27), channel_id=1, source_target_pairs={{0,16},{1,17},{2,18},{3,19},{4,20},{5,21},{6,22},{7,23},{8,24},{9,... | collective-permute-start | bytes 1474568 | tf_op jit(solution)/shard_map/ppermute | solution.py:153
  94.2 14.9 %collective-permute-start.12 = (bf16[24,40,256]{2,1,0:T(8,128)(2,1)S(1)}, bf16[24,40,256]{2,1,0:T(8,128)(2,1)S(1)}, u32[]{:S(2)}, u32[]{:S(2)}) collective-permute-start(bf16[24,40,256]{2,1,0:T(8,128)(2,1)S(1)} %get-tuple-element.28), channel_id=1, source_target_pairs={{16,0},{17,1},{18,2},{19,3},{20,4},{21,5},{22,6},{23,7},{24,8},{25... | collective-permute-start | bytes 1474568 | tf_op jit(solution)/shard_map/ppermute | solution.py:158

commit v3 on v2

--- a/solution.py
+++ b/solution.py
@@ -10,7 +10,7 @@
 HALF_LAT = 24
 POLAR = 64
 X_RUN = 4
-HELPERS = {0: (10, 26, 17, 18), 1: (1, 9, 25, 2), 30: (30, 22, 6, 29), 31: (21, 5, 14, 13)}
+HELPERS = {0: (2, 10, 26, 18), 1: (1, 9, 25, 17), 30: (30, 22, 6, 14), 31: (29, 21, 5, 13)}
 TILE = 128
 
 
@@ -203,6 +203,7 @@
     handed = [
         lax.ppermute(data[q * share : (q + 1) * share], axes, pairs(hands(q))) for q in range(shares)
     ]
+    handed[1], late = lax.optimization_barrier((handed[1], data))
     given = jnp.where(keeps, data[:share], sum(handed))
     parts = given.reshape(lon_count, member_count // pieces, lon_cols)
 
@@ -210,7 +211,7 @@
         data, axes, pairs(lambda lat, lon: None if polar_of(lat) else (lat, lon + 1))
     )
     right = lax.ppermute(
-        data, axes, pairs(lambda lat, lon: None if polar_of(lat) else (lat, lon - 1))
+        late, axes, pairs(lambda lat, lon: None if polar_of(lat) else (lat, lon - 1))
     )
     widths = lax.dynamic_slice_in_dim(support, lat_index * lat_rows, lat_rows).astype(jnp.float32)
     unit_width = lax.dynamic_slice_in_dim(support, row_of + lon_index // pieces, 1).astype(jnp.float32)

time: 111 us -> 107 us (0.964)
  waiting for transfers between devices: 69.7 us -> 67 us
  starting transfers between devices: 26.3 us -> 24.7 us
    ppermute x4, waiting for transfers between devices: 54 us -> 51 us  [body(): polar = [lax.ppermute(done, axes, pairs(returns(q))) for q in range(shares)]]
    ppermute x4, starting transfers between devices: 16.5 us -> 14.8 us  [body(): lax.ppermute(data[q * share:(q + 1) * share], axes, pairs(hands(q)))]
  transfers between devices with their start and end apart: 13 -> 13, of which waited for: 4 -> 5; matrix products, arithmetic and copies ran while one was open for 5% -> 5% of each run, Pallas kernels for 4% -> 4%
where the time goes in v3:
time: 107 us; the launch traced here: 106 us
  waiting for transfers between devices  67 us (63%)
  starting transfers between devices  24.7 us (23%)
  local copies, waits for them, and re-layouts  5.2 us (5%)
  Pallas kernels  4.04 us (4%)
  other arithmetic  1.92 us (2%)
  matrix products  1.88 us (2%)
  between operations  1.63 us (2%)
    ppermute x4, waiting for transfers between devices, body(): polar = [lax.ppermute(done, axes, pairs(returns(q))) for q in range(shares)]  51 us
    ppermute x4, starting transfers between devices, body(): lax.ppermute(data[q * share:(q + 1) * share], axes, pairs(hands(q)))  14.8 us
    ppermute x1, waiting for transfers between devices, next_halo(): lax.ppermute(along[-HALF_LAT:], axes, pairs(lambda lat, lon: (lat + 1, lo...  8.95 us
    ppermute x4, starting transfers between devices, body(): polar = [lax.ppermute(done, axes, pairs(returns(q))) for q in range(shares)]  5.17 us
    pallas_call x1, Pallas kernels, near_product(): pl.pallas_call(near_kernel, grid=(rows // step,), in_specs=[smem, smem, b...  4.04 us
    ppermute x1, waiting for transfers between devices, next_halo(): lax.ppermute(along[:HALF_LAT], axes, pairs(lambda lat, lon: (lat - 1, lon...  3.94 us
    ppermute x4, waiting for transfers between devices, body(): lax.ppermute(data[q * share:(q + 1) * share], axes, pairs(hands(q)))  3.18 us
  transfers between devices with their start and end apart: 13, of which 5 were waited for; matrix products, arithmetic and copies ran while one was open for 5% of the time, Pallas kernels for 4%

profile of v3, /device:TPU:1, one launch (start us, length us, event | category | flops | bytes accessed | tf_op | source)
XLA Modules:
  0.0 106.4 jit_solution(202933712520799747)
XLA Ops:
  0.0 1.5 %copy.18 = bf16[40,32,256]{2,0,1:T(8,128)(2,1)S(1)} copy(bf16[40,32,256]{2,1,0:T(8,128)(2,1)} %param.5) | data formatting | bytes 1310720 | tf_op args[0]
  1.5 0.7 collective-permute-start.4
  2.2 9.9 %collective-permute-start.1 = (bf16[8,40,256]{2,1,0:T(8,128)(2,1)S(1)}, bf16[8,40,256]{2,1,0:T(8,128)(2,1)S(1)}, u32[]{:S(2)}, u32[]{:S(2)}) collective-permute-start(bf16[8,40,256]{2,1,0:T(8,128)(2,1)S(1)} %get-tuple-element.33), channel_id=1, source_target_pairs={{0,160},{1,161},{2,162},{3,163},{4,164},{5,165},{6,166},{7,167},{8... | collective-permute-start | bytes 491528 | tf_op jit(solution)/shard_map/ppermute | solution.py:204
  12.1 2.3 %collective-permute-start.3 = (bf16[8,40,256]{2,1,0:T(8,128)(2,1)S(1)}, bf16[8,40,256]{2,1,0:T(8,128)(2,1)S(1)}, u32[]{:S(2)}, u32[]{:S(2)}) collective-permute-start(bf16[8,40,256]{2,1,0:T(8,128)(2,1)S(1)} %get-tuple-element.34), channel_id=1, source_target_pairs={{0,288},{1,289},{2,290},{3,291},{4,292},{5,293},{6,294},{7,295},{8... | collective-permute-start | bytes 491528 | tf_op jit(solution)/shard_map/ppermute | solution.py:204
  14.4 1.3 %collective-permute-start.2 = (bf16[8,40,256]{2,1,0:T(8,128)(2,1)S(1)}, bf16[8,40,256]{2,1,0:T(8,128)(2,1)S(1)}, u32[]{:S(2)}, u32[]{:S(2)}) collective-permute-start(bf16[8,40,256]{2,1,0:T(8,128)(2,1)S(1)} %get-tuple-element.35), channel_id=1, source_target_pairs={{0,416},{1,417},{2,418},{3,419},{4,420},{5,421},{6,422},{7,423},{8... | collective-permute-start | bytes 491528 | tf_op jit(solution)/shard_map/ppermute | solution.py:204
  15.7 1.3 %collective-permute-start = (bf16[8,40,256]{2,1,0:T(8,128)(2,1)S(1)}, bf16[8,40,256]{2,1,0:T(8,128)(2,1)S(1)}, u32[]{:S(2)}, u32[]{:S(2)}) collective-permute-start(bf16[8,40,256]{2,1,0:T(8,128)(2,1)S(1)} %get-tuple-element.36), channel_id=1, source_target_pairs={{0,32},{1,33},{2,34},{3,35},{4,36},{5,37},{6,38},{7,39},{8,40},{9,... | collective-permute-start | bytes 491528 | tf_op jit(solution)/shard_map/ppermute | solution.py:204
  17.1 0.6 dynamic_slice.10
  18.4 0.8 dynamic-slice_convert_fusion.width_ref
  19.1 1.3 %dynamic_slice.11 = s32[1]{0:T(128)} dynamic-slice(s32[1024]{0:T(1024)} %param.6, s32[]{:T(128)S(6)} %select_n.86), dynamic_slice_sizes={1} | dynamic-slice | bytes 12 | tf_op jit(solution)/shard_map/dynamic_slice | solution.py:217
  21.3 0.7 collective-permute-start.5
  22.0 0.3 fusion.6
  22.4 0.7 collective-permute-done.2
  23.2 2.5 %collective-permute-done = bf16[8,40,256]{2,1,0:T(8,128)(2,1)S(1)} collective-permute-done((bf16[8,40,256]{2,1,0:T(8,128)(2,1)S(1)}, bf16[8,40,256]{2,1,0:T(8,128)(2,1)S(1)}, u32[]{:S(2)}, u32[]{:S(2)}) %collective-permute-start) | collective-permute-done | bytes 163872 | tf_op jit(solution)/shard_map/ppermute | solution.py:204
  25.7 0.7 reshape.69
  26.4 1.0 reshape.70
  27.4 1.3 %collective-permute-start.10 = (bf16[8,40,256]{2,1,0:T(8,128)(2,1)S(1)}, bf16[8,40,256]{2,1,0:T(8,128)(2,1)S(1)}, u32[]{:S(2)}, u32[]{:S(2)}) collective-permute-start(bf16[8,40,256]{2,1,0:T(8,128)(2,1)S(1)} %reshape.70), channel_id=1, source_target_pairs={{208,496},{209,497},{210,498},{211,499},{212,500},{213,501},{214,5... | collective-permute-start | bytes 491528 | tf_op jit(solution)/shard_map/ppermute | solution.py:231
  28.7 1.3 %collective-permute-start.9 = (bf16[8,40,256]{2,1,0:T(8,128)(2,1)S(1)}, bf16[8,40,256]{2,1,0:T(8,128)(2,1)S(1)}, u32[]{:S(2)}, u32[]{:S(2)}) collective-permute-start(bf16[8,40,256]{2,1,0:T(8,128)(2,1)S(1)} %reshape.70), channel_id=1, source_target_pairs={{80,496},{81,497},{82,498},{83,499},{84,500},{85,501},{86,502},{87... | collective-permute-start | bytes 491528 | tf_op jit(solution)/shard_map/ppermute | solution.py:231
  30.0 1.3 %collective-permute-start.8 = (bf16[8,40,256]{2,1,0:T(8,128)(2,1)S(1)}, bf16[8,40,256]{2,1,0:T(8,128)(2,1)S(1)}, u32[]{:S(2)}, u32[]{:S(2)}) collective-permute-start(bf16[8,40,256]{2,1,0:T(8,128)(2,1)S(1)} %reshape.70), channel_id=1, source_target_pairs={{144,16},{145,17},{146,18},{147,19},{148,20},{149,21},{150,22},{15... | collective-permute-start | bytes 491528 | tf_op jit(solution)/shard_map/ppermute | solution.py:231
  31.3 1.3 %collective-permute-start.7 = (bf16[8,40,256]{2,1,0:T(8,128)(2,1)S(1)}, bf16[8,40,256]{2,1,0:T(8,128)(2,1)S(1)}, u32[]{:S(2)}, u32[]{:S(2)}) collective-permute-start(bf16[8,40,256]{2,1,0:T(8,128)(2,1)S(1)} %reshape.70), channel_id=1, source_target_pairs={{32,0},{33,1},{34,2},{35,3},{36,4},{37,5},{38,6},{39,7},{40,8},{41... | collective-permute-start | bytes 491528 | tf_op jit(solution)/shard_map/ppermute | solution.py:231
  32.6 4.0 %shard_map.37 = bf16[32,40,256]{2,1,0:T(8,128)(2,1)S(1)} custom-call(f32[32]{0:T(128)S(1)} %dynamic-slice_convert_fusion.width_ref, f32[32]{0:T(128)S(1)} %bitcast.28, bf16[32,40,256]{2,1,0:T(8,128)(2,1)S(1)} %collective-permute-done.4.left_ref, bf16[32,40,256]{2,1,0:T(8,128)(2,1)S(1)} %bitcast.25, bf16[32,40,256]{2,1,0:T(8,128)(2,1)S(1)} %collective-permute-done.5.right_ref), custom_call_target="tpu_custom_call" | custom-call | tf_op jit(solution)/shard_map/pallas_call | solution.py:66
  36.6 0.7 collective-permute-start.6
  37.3 51.0 %collective-permute-done.7 = bf16[8,40,256]{2,1,0:T(8,128)(2,1)S(1)} collective-permute-done((bf16[8,40,256]{2,1,0:T(8,128)(2,1)S(1)}, bf16[8,40,256]{2,1,0:T(8,128)(2,1)S(1)}, u32[]{:S(2)}, u32[]{:S(2)}) %collective-permute-start.7) | collective-permute-done | bytes 163872 | tf_op jit(solution)/shard_map/ppermute | solution.py:231
  88.4 0.1 maximum_select_fusion
  88.6 1.3 %collective-permute-start.11 = (bf16[24,40,256]{2,1,0:T(8,128)(2,1)S(1)}, bf16[24,40,256]{2,1,0:T(8,128)(2,1)S(1)}, u32[]{:S(2)}, u32[]{:S(2)}) collective-permute-start(bf16[24,40,256]{2,1,0:T(8,128)(2,1)S(1)} %get-tuple-element.31), channel_id=1, source_target_pairs={{0,16},{1,17},{2,18},{3,19},{4,20},{5,21},{6,22},{7,23},{8,24},{9,... | collective-permute-start | bytes 1474568 | tf_op jit(solution)/shard_map/ppermute | solution.py:153
  89.9 1.3 %collective-permute-start.12 = (bf16[24,40,256]{2,1,0:T(8,128)(2,1)S(1)}, bf16[24,40,256]{2,1,0:T(8,128)(2,1)S(1)}, u32[]{:S(2)}, u32[]{:S(2)}) collective-permute-start(bf16[24,40,256]{2,1,0:T(8,128)(2,1)S(1)} %get-tuple-element.32), channel_id=1, source_target_pairs={{16,0},{17,1},{18,2},{19,3},{20,4},{21,5},{22,6},{23,7},{24,8},{25... | collective-permute-start | bytes 1474568 | tf_op jit(solution)/shard_map/ppermute | solution.py:158
  91.2 0.2 select_reduce_fusion
  91.4 0.1 pad_maximum_fusion
  91.5 0.4 convolution_bitcast_fusion.1
  91.9 8.9 %collective-permute-done.11 = bf16[24,40,256]{2,1,0:T(8,128)(2,1)S(1)} collective-permute-done((bf16[24,40,256]{2,1,0:T(8,128)(2,1)S(1)}, bf16[24,40,256]{2,1,0:T(8,128)(2,1)S(1)}, u32[]{:S(2)}, u32[]{:S(2)}) %collective-permute-start.11) | collective-permute-done | bytes 491552 | tf_op jit(solution)/shard_map/ppermute | solution.py:153
  100.9 3.9 %collective-permute-done.12 = bf16[24,40,256]{2,1,0:T(8,128)(2,1)S(1)} collective-permute-done((bf16[24,40,256]{2,1,0:T(8,128)(2,1)S(1)}, bf16[24,40,256]{2,1,0:T(8,128)(2,1)S(1)}, u32[]{:S(2)}, u32[]{:S(2)}) %collective-permute-start.12) | collective-permute-done | bytes 491552 | tf_op jit(solution)/shard_map/ppermute | solution.py:158
  104.8 0.1 pad_maximum_fusion.1
  104.9 1.5 %fusion.1 = f32[40,32,256]{2,1,0:T(8,128)} fusion(f32[40,32,256]{2,1,0:T(8,128)S(1)} %convolution_bitcast_fusion.1, bf16[48,40,256]{2,1,0:T(8,128)(2,1)S(1)} %pad_maximum_fusion.1, f32[32]{0:T(128)S(1)} %sqrt.7, bf16[24,32]{0,1:T(8,128)(2,1)S(1)} %get-tuple-element.39, bf16[24,32]{0,1:T(8,128)(2,1)S(1)} %get-tuple-element.37), kind=kOutput, calls=%fused_computation.2 | convolution fusion | flops 32118784 | bytes 3607680 | tf_op jit(solution)/shard_map/jmc,jr->mrc/dot_general | solution.py:263
  (28 shorter events, 0.5 us)
Async XLA Ops:
  0.0 17.1 %copy-start = (s32[32]{0:T(128)S(1)}, s32[32]{0:T(128)}, u32[]{:S(2)}) copy-start(s32[32]{0:T(128)} %constant.105.clone) | copy-start | bytes 388
  1.5 24.9 %collective-permute-start.4 = (bf16[32,40,256]{2,1,0:T(8,128)(2,1)S(1)}, bf16[32,40,256]{2,1,0:T(8,128)(2,1)S(1)}, u32[]{:S(2)}, u32[]{:S(2)}) collective-permute-start(bf16[32,40,256]{2,1,0:T(8,128)(2,1)S(1)} %bitcast.21), channel_id=1, source_target_pairs={{32,33},{33,34},{34,35},{35,36},{36,37},{37,38},{38,39},{39,40},{4... | collective-permute-start | bytes 1966088 | tf_op jit(solution)/shard_map/ppermute | solution.py:210
  2.2 19.0 %collective-permute-start.1 = (bf16[8,40,256]{2,1,0:T(8,128)(2,1)S(1)}, bf16[8,40,256]{2,1,0:T(8,128)(2,1)S(1)}, u32[]{:S(2)}, u32[]{:S(2)}) collective-permute-start(bf16[8,40,256]{2,1,0:T(8,128)(2,1)S(1)} %get-tuple-element.33), channel_id=1, source_target_pairs={{0,160},{1,161},{2,162},{3,163},{4,164},{5,165},{6,166},{7,167},{8... | collective-permute-start | bytes 491528 | tf_op jit(solution)/shard_map/ppermute | solution.py:204
  12.1 10.3 %collective-permute-start.3 = (bf16[8,40,256]{2,1,0:T(8,128)(2,1)S(1)}, bf16[8,40,256]{2,1,0:T(8,128)(2,1)S(1)}, u32[]{:S(2)}, u32[]{:S(2)}) collective-permute-start(bf16[8,40,256]{2,1,0:T(8,128)(2,1)S(1)} %get-tuple-element.34), channel_id=1, source_target_pairs={{0,288},{1,289},{2,290},{3,291},{4,292},{5,293},{6,294},{7,295},{8... | collective-permute-start | bytes 491528 | tf_op jit(solution)/shard_map/ppermute | solution.py:204
  14.4 8.7 %collective-permute-start.2 = (bf16[8,40,256]{2,1,0:T(8,128)(2,1)S(1)}, bf16[8,40,256]{2,1,0:T(8,128)(2,1)S(1)}, u32[]{:S(2)}, u32[]{:S(2)}) collective-permute-start(bf16[8,40,256]{2,1,0:T(8,128)(2,1)S(1)} %get-tuple-element.35), channel_id=1, source_target_pairs={{0,416},{1,417},{2,418},{3,419},{4,420},{5,421},{6,422},{7,423},{8... | collective-permute-start | bytes 491528 | tf_op jit(solution)/shard_map/ppermute | solution.py:204
  15.7 9.9 %collective-permute-start = (bf16[8,40,256]{2,1,0:T(8,128)(2,1)S(1)}, bf16[8,40,256]{2,1,0:T(8,128)(2,1)S(1)}, u32[]{:S(2)}, u32[]{:S(2)}) collective-permute-start(bf16[8,40,256]{2,1,0:T(8,128)(2,1)S(1)} %get-tuple-element.36), channel_id=1, source_target_pairs={{0,32},{1,33},{2,34},{3,35},{4,36},{5,37},{6,38},{7,39},{8,40},{9,... | collective-permute-start | bytes 491528 | tf_op jit(solution)/shard_map/ppermute | solution.py:204
  21.3 5.1 %collective-permute-start.5 = (bf16[32,40,256]{2,1,0:T(8,128)(2,1)S(1)}, bf16[32,40,256]{2,1,0:T(8,128)(2,1)S(1)}, u32[]{:S(2)}, u32[]{:S(2)}) collective-permute-start(bf16[32,40,256]{2,1,0:T(8,128)(2,1)S(1)} %bitcast.23), channel_id=1, source_target_pairs={{32,47},{33,32},{34,33},{35,34},{36,35},{37,36},{38,37},{39,38},{4... | collective-permute-start | bytes 1966088 | tf_op jit(solution)/shard_map/ppermute | solution.py:213
  27.4 61.0 %collective-permute-start.10 = (bf16[8,40,256]{2,1,0:T(8,128)(2,1)S(1)}, bf16[8,40,256]{2,1,0:T(8,128)(2,1)S(1)}, u32[]{:S(2)}, u32[]{:S(2)}) collective-permute-start(bf16[8,40,256]{2,1,0:T(8,128)(2,1)S(1)} %reshape.70), channel_id=1, source_target_pairs={{208,496},{209,497},{210,498},{211,499},{212,500},{213,501},{214,5... | collective-permute-start | bytes 491528 | tf_op jit(solution)/shard_map/ppermute | solution.py:231
  28.7 59.7 %collective-permute-start.9 = (bf16[8,40,256]{2,1,0:T(8,128)(2,1)S(1)}, bf16[8,40,256]{2,1,0:T(8,128)(2,1)S(1)}, u32[]{:S(2)}, u32[]{:S(2)}) collective-permute-start(bf16[8,40,256]{2,1,0:T(8,128)(2,1)S(1)} %reshape.70), channel_id=1, source_target_pairs={{80,496},{81,497},{82,498},{83,499},{84,500},{85,501},{86,502},{87... | collective-permute-start | bytes 491528 | tf_op jit(solution)/shard_map/ppermute | solution.py:231
  30.0 58.4 %collective-permute-start.8 = (bf16[8,40,256]{2,1,0:T(8,128)(2,1)S(1)}, bf16[8,40,256]{2,1,0:T(8,128)(2,1)S(1)}, u32[]{:S(2)}, u32[]{:S(2)}) collective-permute-start(bf16[8,40,256]{2,1,0:T(8,128)(2,1)S(1)} %reshape.70), channel_id=1, source_target_pairs={{144,16},{145,17},{146,18},{147,19},{148,20},{149,21},{150,22},{15... | collective-permute-start | bytes 491528 | tf_op jit(solution)/shard_map/ppermute | solution.py:231
  31.3 57.0 %collective-permute-start.7 = (bf16[8,40,256]{2,1,0:T(8,128)(2,1)S(1)}, bf16[8,40,256]{2,1,0:T(8,128)(2,1)S(1)}, u32[]{:S(2)}, u32[]{:S(2)}) collective-permute-start(bf16[8,40,256]{2,1,0:T(8,128)(2,1)S(1)} %reshape.70), channel_id=1, source_target_pairs={{32,0},{33,1},{34,2},{35,3},{36,4},{37,5},{38,6},{39,7},{40,8},{41... | collective-permute-start | bytes 491528 | tf_op jit(solution)/shard_map/ppermute | solution.py:231
  36.6 54.7 %collective-permute-start.6 = (bf16[24,40,256]{2,1,0:T(8,128)(2,1)S(1)}, bf16[24,40,256]{2,1,0:T(8,128)(2,1)S(1)}, u32[]{:S(2)}, u32[]{:S(2)}) collective-permute-start(bf16[24,40,256]{2,1,0:T(8,128)(2,1)S(1)} %slice_select_fusion), channel_id=1, source_target_pairs={{48,64},{49,65},{50,66},{51,67},{52,68},{53,69},{54,70},{55,71},{5... | collective-permute-start | bytes 1474568 | tf_op jit(solution)/shard_map/ppermute | solution.py:146
  88.6 12.3 %collective-permute-start.11 = (bf16[24,40,256]{2,1,0:T(8,128)(2,1)S(1)}, bf16[24,40,256]{2,1,0:T(8,128)(2,1)S(1)}, u32[]{:S(2)}, u32[]{:S(2)}) collective-permute-start(bf16[24,40,256]{2,1,0:T(8,128)(2,1)S(1)} %get-tuple-element.31), channel_id=1, source_target_pairs={{0,16},{1,17},{2,18},{3,19},{4,20},{5,21},{6,22},{7,23},{8,24},{9,... | collective-permute-start | bytes 1474568 | tf_op jit(solution)/shard_map/ppermute | solution.py:153
  89.9 14.9 %collective-permute-start.12 = (bf16[24,40,256]{2,1,0:T(8,128)(2,1)S(1)}, bf16[24,40,256]{2,1,0:T(8,128)(2,1)S(1)}, u32[]{:S(2)}, u32[]{:S(2)}) collective-permute-start(bf16[24,40,256]{2,1,0:T(8,128)(2,1)S(1)} %get-tuple-element.32), channel_id=1, source_target_pairs={{16,0},{17,1},{18,2},{19,3},{20,4},{21,5},{22,6},{23,7},{24,8},{25... | collective-permute-start | bytes 1474568 | tf_op jit(solution)/shard_map/ppermute | solution.py:158

commit v4 on v3

--- a/solution.py
+++ b/solution.py
@@ -1,4 +1,5 @@
 import functools
+import math
 
 import jax
 import jax.numpy as jnp
@@ -12,6 +13,7 @@
 X_RUN = 4
 HELPERS = {0: (2, 10, 26, 18), 1: (1, 9, 25, 17), 30: (30, 22, 6, 14), 31: (29, 21, 5, 13)}
 TILE = 128
+LOG2E = math.log2(math.e)
 
 
 def flat_pairs(lat_count, lon_count, target):
@@ -24,43 +26,38 @@
     return pairs
 
 
-def toeplitz(offset, square, falloff, scale, nlon_all=None):
-    distance = jnp.abs(offset)
-    if nlon_all is not None:
-        distance = jnp.minimum(distance, nlon_all - distance)
-    distance_sq = distance * distance
-    raw = jnp.where(distance_sq <= square, jnp.exp(distance_sq * falloff), 0.0)
-    return (raw * scale).astype(jnp.bfloat16)
-
-
-def near_kernel(width_ref, scale_ref, left_ref, mid_ref, right_ref, out_ref):
+def difference(shape):
+    return (lax.broadcasted_iota(jnp.int32, shape, 0) - lax.broadcasted_iota(jnp.int32, shape, 1)).astype(jnp.float32)
+
+def toeplitz(distance_sq, square, falloff, level):
+    value = jnp.exp2(distance_sq * falloff + level)
+    return jnp.where(distance_sq <= square, value, 0.0).astype(jnp.bfloat16)
+
+
+def near_kernel(width_ref, level_ref, left_ref, mid_ref, right_ref, out_ref):
     rows = mid_ref.shape[0]
     first = pl.program_id(0) * rows
-    base = (
-        lax.broadcasted_iota(jnp.int32, (TILE, TILE), 0)
-        - lax.broadcasted_iota(jnp.int32, (TILE, TILE), 1)
-    ).astype(jnp.float32)
-    zero = jnp.zeros((TILE, TILE), jnp.bfloat16)
+    base = difference((TILE, TILE))
+    distances = {k: (base + float(k * TILE)) * (base + float(k * TILE)) for k in range(-2, 3)}
     for row in range(rows):
         width = width_ref[first + row]
-        scale = scale_ref[first + row]
+        level = level_ref[first + row]
         square = width * width
-        falloff = -2.0 / square
-        t = {3: zero, -3: zero}
+        falloff = (-2.0 * LOG2E) / square
+        t = {}
         for k in range(-2, 3):
-            t[k] = toeplitz(base + float(k * TILE), square, falloff, scale)
-        weights = jnp.concatenate(
-            [jnp.concatenate([t[a - 2], t[a - 3]], axis=1) for a in range(6)], axis=0
-        )
+            t[k] = toeplitz(distances[k], square, falloff, level)
+        weights = jnp.concatenate([t[k] for k in range(-2, 3)], axis=0)
         data = jnp.concatenate([left_ref[row], mid_ref[row], right_ref[row]], axis=1)
-        out_ref[row] = jnp.dot(data, weights, preferred_element_type=jnp.float32).astype(
-            jnp.bfloat16
-        )
-
-
-def near_product(left, mid, right, widths, scales):
+        both = jnp.concatenate([data[:, : 5 * TILE], data[:, TILE:]], axis=0)
+        got = jnp.dot(both, weights, preferred_element_type=jnp.float32).astype(jnp.bfloat16)
+        half = data.shape[0]
+        out_ref[row] = jnp.concatenate([got[:half], got[half:]], axis=1)
+
+
+def near_product(left, mid, right, widths, levels):
     rows, members, cols = mid.shape
-    step = 8
+    step = 16
     block = pl.BlockSpec((step, members, cols), lambda i: (i, 0, 0))
     smem = pl.BlockSpec(memory_space=pltpu.SMEM)
     return pl.pallas_call(
@@ -70,52 +67,65 @@
         out_specs=block,
         out_shape=jax.ShapeDtypeStruct(mid.shape, jnp.bfloat16),
         compiler_params=pltpu.CompilerParams(vmem_limit_bytes=48 * 1024 * 1024),
-    )(widths, scales, left, mid, right)
-
-
-def circle_kernel(blocks, width_ref, scale_ref, data_ref, out_ref, twice, total):
-    size, cols = data_ref.shape[1:]
-    span = size // blocks
-    nlon_all = float(blocks * cols)
-    base = (
-        lax.broadcasted_iota(jnp.int32, (cols, cols), 0)
-        - lax.broadcasted_iota(jnp.int32, (cols, cols), 1)
-    ).astype(jnp.float32)
-    for row in range(data_ref.shape[0]):
-        twice[:size] = data_ref[row]
-        twice[size:] = data_ref[row]
-        width = width_ref[row]
-        scale = scale_ref[row]
-        square = width * width
-        falloff = -2.0 / square
-        total[...] = jnp.zeros_like(total)
-
-        def step(k, carry):
-            offset = base + (k * cols).astype(jnp.float32)
-            weights = toeplitz(offset, square, falloff, scale, nlon_all)
-            data = twice[pl.ds(pl.multiple_of(k * span, 16), size)]
-            total[...] += jnp.dot(data, weights, preferred_element_type=jnp.float32)
-            return carry
-
-        lax.fori_loop(0, blocks, step, 0, unroll=4)
-        out_ref[row] = total[...].astype(jnp.bfloat16)
-
-
-def circle_product(data, widths, scales, blocks):
-    rows, size, cols = data.shape
+    )(widths, levels, left, mid, right)
+
+
+def circle_kernel(width_ref, level_ref, data_ref, out_ref, tiles, twice, total):
+    blocks, members, cols = data_ref.shape
+    span = twice.shape[0] // (2 * blocks)
+    size = blocks * span
+    count = blocks * cols // TILE
+    base = difference((TILE, TILE))
+    width = width_ref[0]
+    level = level_ref[0]
+    square = width * width
+    falloff = (-2.0 * LOG2E) / square
+    for n in range(count // 2 + 1):
+        distance = jnp.abs(base + float(n * TILE))
+        distance = jnp.minimum(distance, float(count * TILE) - distance)
+        tile = toeplitz(distance * distance, square, falloff, level)
+        tiles[n] = tile
+        if 0 < n < count // 2:
+            tiles[count - n] = tile.T
+    pad = jnp.zeros((span - members, cols), jnp.bfloat16)
+    for i in range(blocks):
+        block = jnp.concatenate([data_ref[i], pad], axis=0)
+        twice[i * span : (i + 1) * span] = block
+        twice[size + i * span : size + (i + 1) * span] = block
+    for k in range(blocks):
+        weights = jnp.concatenate(
+            [
+                jnp.concatenate([tiles[2 * k], tiles[(2 * k - 1) % count]], axis=1),
+                jnp.concatenate([tiles[(2 * k + 1) % count], tiles[2 * k]], axis=1),
+            ],
+            axis=0,
+        )
+        part = jnp.dot(twice[k * span : k * span + size], weights, preferred_element_type=jnp.float32)
+        if k == 0:
+            total[...] = part
+        else:
+            total[...] += part
+    for i in range(blocks):
+        out_ref[i] = total[i * span : i * span + members].astype(jnp.bfloat16)
+
+
+def unit_product(parts, width, level):
+    blocks, members, cols = parts.shape
+    span = members + -members % 16
     smem = pl.BlockSpec(memory_space=pltpu.SMEM)
     vmem = pl.BlockSpec(memory_space=pltpu.VMEM)
     return pl.pallas_call(
-        functools.partial(circle_kernel, blocks),
+        circle_kernel,
         in_specs=[smem, smem, vmem],
         out_specs=vmem,
-        out_shape=jax.ShapeDtypeStruct(data.shape, jnp.bfloat16),
+        out_shape=jax.ShapeDtypeStruct(parts.shape, jnp.bfloat16),
         scratch_shapes=[
-            pltpu.VMEM((2 * size, cols), jnp.bfloat16),
-            pltpu.VMEM((size, cols), jnp.float32),
+            pltpu.VMEM((blocks * cols // TILE, TILE, TILE), jnp.bfloat16),
+            pltpu.VMEM((2 * blocks * span, cols), jnp.bfloat16),
+            pltpu.VMEM((blocks * span, cols), jnp.float32),
         ],
         compiler_params=pltpu.CompilerParams(vmem_limit_bytes=48 * 1024 * 1024),
-    )(widths, scales, data)
+    )(width, level, parts)
 
 
 def row_scale(width_f, nlon_all):
@@ -126,14 +136,6 @@
         distance <= width_f, jnp.exp(-2.0 * distance * distance / (width_f * width_f)), 0.0
     )
     return 1.0 / jnp.sqrt(jnp.sum(weights_raw * weights_raw, axis=1))
-
-
-def unit_product(parts, width, scale):
-    blocks, members, cols = parts.shape
-    padded = members + -members % 16
-    data = jnp.pad(parts, ((0, 0), (0, padded - members), (0, 0)))
-    result = circle_product(data.reshape(1, blocks * padded, cols), width, scale, blocks)
-    return result.reshape(blocks, padded, cols)[:, :members]
 
 
 def far_halo(near, lat_index, lat_count, lon_count):
@@ -215,16 +217,16 @@
     )
     widths = lax.dynamic_slice_in_dim(support, lat_index * lat_rows, lat_rows).astype(jnp.float32)
     unit_width = lax.dynamic_slice_in_dim(support, row_of + lon_index // pieces, 1).astype(jnp.float32)
-    scales = row_scale(jnp.concatenate([widths, unit_width]), nlon_all)
-    scales, unit_scale = scales[:lat_rows], scales[lat_rows:]
+    levels = jnp.log2(row_scale(jnp.concatenate([widths, unit_width]), nlon_all))
+    levels, unit_level = levels[:lat_rows], levels[lat_rows:]
 
     def helping(parts):
         parts = lax.all_to_all(parts, "lon", 0, 0)
-        return lax.all_to_all(unit_product(parts, unit_width, unit_scale), "lon", 0, 0)
+        return lax.all_to_all(unit_product(parts, unit_width, unit_level), "lon", 0, 0)
 
     parts = lax.cond(takes_part, helping, lambda v: v, parts)
     parts, left, right = lax.optimization_barrier((parts, left, right))
-    near = near_product(left, data, right, widths, scales)
+    near = near_product(left, data, right, widths, levels)
 
     far = far_halo(near, lat_index, lat_count, lon_count)
     done = parts.reshape(share, member_count, lon_cols)

time: 107 us -> 106 us (level)
  transfers between devices with their start and end apart: 13 -> 13, of which waited for: 5 -> 5; matrix products, arithmetic and copies ran while one was open for 5% -> 5% of each run, Pallas kernels for 4% -> 3%
where the time goes in v4:
time: 106 us; the launch traced here: 105 us
  waiting for transfers between devices  66.6 us (63%)
  starting transfers between devices  24.7 us (23%)
  local copies, waits for them, and re-layouts  5.2 us (5%)
  Pallas kernels  3.18 us (3%)
  other arithmetic  1.93 us (2%)
  matrix products  1.88 us (2%)
  between operations  1.64 us (2%)
    ppermute x4, waiting for transfers between devices, body(): polar = [lax.ppermute(done, axes, pairs(returns(q))) for q in range(shares)]  50.5 us
    ppermute x4, starting transfers between devices, body(): lax.ppermute(data[q * share:(q + 1) * share], axes, pairs(hands(q)))  14.8 us
    ppermute x1, waiting for transfers between devices, next_halo(): lax.ppermute(along[-HALF_LAT:], axes, pairs(lambda lat, lon: (lat + 1, lo...  8.95 us
    ppermute x4, starting transfers between devices, body(): polar = [lax.ppermute(done, axes, pairs(returns(q))) for q in range(shares)]  5.17 us
    ppermute x1, waiting for transfers between devices, next_halo(): lax.ppermute(along[:HALF_LAT], axes, pairs(lambda lat, lon: (lat - 1, lon...  3.94 us
    pallas_call x1, Pallas kernels, near_product(): pl.pallas_call(near_kernel, grid=(rows // step,), in_specs=[smem, smem, b...  3.18 us
    ppermute x4, waiting for transfers between devices, body(): lax.ppermute(data[q * share:(q + 1) * share], axes, pairs(hands(q)))  3.17 us
  transfers between devices with their start and end apart: 13, of which 5 were waited for; matrix products, arithmetic and copies ran while one was open for 5% of the time, Pallas kernels for 3%

profile of v4, /device:TPU:1, one launch (start us, length us, event | category | flops | bytes accessed | tf_op | source)
XLA Modules:
  0.0 105.1 jit_solution(3670925543365160646)
XLA Ops:
  0.0 1.5 %copy.18 = bf16[40,32,256]{2,0,1:T(8,128)(2,1)S(1)} copy(bf16[40,32,256]{2,1,0:T(8,128)(2,1)} %param.5) | data formatting | bytes 1310720 | tf_op args[0]
  1.5 0.7 collective-permute-start.4
  2.2 9.9 %collective-permute-start.1 = (bf16[8,40,256]{2,1,0:T(8,128)(2,1)S(1)}, bf16[8,40,256]{2,1,0:T(8,128)(2,1)S(1)}, u32[]{:S(2)}, u32[]{:S(2)}) collective-permute-start(bf16[8,40,256]{2,1,0:T(8,128)(2,1)S(1)} %get-tuple-element.33), channel_id=1, source_target_pairs={{0,160},{1,161},{2,162},{3,163},{4,164},{5,165},{6,166},{7,167},{8... | collective-permute-start | bytes 491528 | tf_op jit(solution)/shard_map/ppermute | solution.py:206
  12.1 2.3 %collective-permute-start.3 = (bf16[8,40,256]{2,1,0:T(8,128)(2,1)S(1)}, bf16[8,40,256]{2,1,0:T(8,128)(2,1)S(1)}, u32[]{:S(2)}, u32[]{:S(2)}) collective-permute-start(bf16[8,40,256]{2,1,0:T(8,128)(2,1)S(1)} %get-tuple-element.34), channel_id=1, source_target_pairs={{0,288},{1,289},{2,290},{3,291},{4,292},{5,293},{6,294},{7,295},{8... | collective-permute-start | bytes 491528 | tf_op jit(solution)/shard_map/ppermute | solution.py:206
  14.4 1.3 %collective-permute-start.2 = (bf16[8,40,256]{2,1,0:T(8,128)(2,1)S(1)}, bf16[8,40,256]{2,1,0:T(8,128)(2,1)S(1)}, u32[]{:S(2)}, u32[]{:S(2)}) collective-permute-start(bf16[8,40,256]{2,1,0:T(8,128)(2,1)S(1)} %get-tuple-element.35), channel_id=1, source_target_pairs={{0,416},{1,417},{2,418},{3,419},{4,420},{5,421},{6,422},{7,423},{8... | collective-permute-start | bytes 491528 | tf_op jit(solution)/shard_map/ppermute | solution.py:206
  15.7 1.3 %collective-permute-start = (bf16[8,40,256]{2,1,0:T(8,128)(2,1)S(1)}, bf16[8,40,256]{2,1,0:T(8,128)(2,1)S(1)}, u32[]{:S(2)}, u32[]{:S(2)}) collective-permute-start(bf16[8,40,256]{2,1,0:T(8,128)(2,1)S(1)} %get-tuple-element.36), channel_id=1, source_target_pairs={{0,32},{1,33},{2,34},{3,35},{4,36},{5,37},{6,38},{7,39},{8,40},{9,... | collective-permute-start | bytes 491528 | tf_op jit(solution)/shard_map/ppermute | solution.py:206
  17.1 0.6 dynamic_slice.10
  18.4 0.8 dynamic-slice_convert_fusion.width_ref
  19.2 1.3 %dynamic_slice.11 = s32[1]{0:T(128)} dynamic-slice(s32[1024]{0:T(1024)} %param.6, s32[]{:T(128)S(6)} %select_n.86), dynamic_slice_sizes={1} | dynamic-slice | bytes 12 | tf_op jit(solution)/shard_map/dynamic_slice | solution.py:219
  21.3 0.3 fusion.6
  21.6 0.7 collective-permute-start.5
  22.5 0.7 collective-permute-done.2
  23.2 2.5 %collective-permute-done = bf16[8,40,256]{2,1,0:T(8,128)(2,1)S(1)} collective-permute-done((bf16[8,40,256]{2,1,0:T(8,128)(2,1)S(1)}, bf16[8,40,256]{2,1,0:T(8,128)(2,1)S(1)}, u32[]{:S(2)}, u32[]{:S(2)}) %collective-permute-start) | collective-permute-done | bytes 163872 | tf_op jit(solution)/shard_map/ppermute | solution.py:206
  25.7 0.7 reshape.63
  26.4 1.0 reshape.64
  27.4 1.3 %collective-permute-start.10 = (bf16[8,40,256]{2,1,0:T(8,128)(2,1)S(1)}, bf16[8,40,256]{2,1,0:T(8,128)(2,1)S(1)}, u32[]{:S(2)}, u32[]{:S(2)}) collective-permute-start(bf16[8,40,256]{2,1,0:T(8,128)(2,1)S(1)} %reshape.64), channel_id=1, source_target_pairs={{208,496},{209,497},{210,498},{211,499},{212,500},{213,501},{214,5... | collective-permute-start | bytes 491528 | tf_op jit(solution)/shard_map/ppermute | solution.py:233
  28.7 1.3 %collective-permute-start.9 = (bf16[8,40,256]{2,1,0:T(8,128)(2,1)S(1)}, bf16[8,40,256]{2,1,0:T(8,128)(2,1)S(1)}, u32[]{:S(2)}, u32[]{:S(2)}) collective-permute-start(bf16[8,40,256]{2,1,0:T(8,128)(2,1)S(1)} %reshape.64), channel_id=1, source_target_pairs={{80,496},{81,497},{82,498},{83,499},{84,500},{85,501},{86,502},{87... | collective-permute-start | bytes 491528 | tf_op jit(solution)/shard_map/ppermute | solution.py:233
  30.0 1.3 %collective-permute-start.8 = (bf16[8,40,256]{2,1,0:T(8,128)(2,1)S(1)}, bf16[8,40,256]{2,1,0:T(8,128)(2,1)S(1)}, u32[]{:S(2)}, u32[]{:S(2)}) collective-permute-start(bf16[8,40,256]{2,1,0:T(8,128)(2,1)S(1)} %reshape.64), channel_id=1, source_target_pairs={{144,16},{145,17},{146,18},{147,19},{148,20},{149,21},{150,22},{15... | collective-permute-start | bytes 491528 | tf_op jit(solution)/shard_map/ppermute | solution.py:233
  31.3 1.3 %collective-permute-start.7 = (bf16[8,40,256]{2,1,0:T(8,128)(2,1)S(1)}, bf16[8,40,256]{2,1,0:T(8,128)(2,1)S(1)}, u32[]{:S(2)}, u32[]{:S(2)}) collective-permute-start(bf16[8,40,256]{2,1,0:T(8,128)(2,1)S(1)} %reshape.64), channel_id=1, source_target_pairs={{32,0},{33,1},{34,2},{35,3},{36,4},{37,5},{38,6},{39,7},{40,8},{41... | collective-permute-start | bytes 491528 | tf_op jit(solution)/shard_map/ppermute | solution.py:233
  32.6 3.2 %shard_map.37 = bf16[32,40,256]{2,1,0:T(8,128)(2,1)S(1)} custom-call(f32[32]{0:T(128)S(1)} %dynamic-slice_convert_fusion.width_ref, f32[32]{0:T(128)S(1)} %bitcast.24, bf16[32,40,256]{2,1,0:T(8,128)(2,1)S(1)} %collective-permute-done.4.left_ref, bf16[32,40,256]{2,1,0:T(8,128)(2,1)S(1)} %bitcast.23, bf16[32,40,256]{2,1,0:T(8,128)(2,1)S(1)} %collective-permute-done.5.right_ref), custom_call_target="tpu_custom_call" | custom-call | tf_op jit(solution)/shard_map/pallas_call | solution.py:63
  35.8 0.7 collective-permute-start.6
  36.5 50.5 %collective-permute-done.7 = bf16[8,40,256]{2,1,0:T(8,128)(2,1)S(1)} collective-permute-done((bf16[8,40,256]{2,1,0:T(8,128)(2,1)S(1)}, bf16[8,40,256]{2,1,0:T(8,128)(2,1)S(1)}, u32[]{:S(2)}, u32[]{:S(2)}) %collective-permute-start.7) | collective-permute-done | bytes 163872 | tf_op jit(solution)/shard_map/ppermute | solution.py:233
  87.0 0.1 maximum_select_fusion
  87.3 1.3 %collective-permute-start.11 = (bf16[24,40,256]{2,1,0:T(8,128)(2,1)S(1)}, bf16[24,40,256]{2,1,0:T(8,128)(2,1)S(1)}, u32[]{:S(2)}, u32[]{:S(2)}) collective-permute-start(bf16[24,40,256]{2,1,0:T(8,128)(2,1)S(1)} %get-tuple-element.31), channel_id=1, source_target_pairs={{0,16},{1,17},{2,18},{3,19},{4,20},{5,21},{6,22},{7,23},{8,24},{9,... | collective-permute-start | bytes 1474568 | tf_op jit(solution)/shard_map/ppermute | solution.py:155
  88.6 1.3 %collective-permute-start.12 = (bf16[24,40,256]{2,1,0:T(8,128)(2,1)S(1)}, bf16[24,40,256]{2,1,0:T(8,128)(2,1)S(1)}, u32[]{:S(2)}, u32[]{:S(2)}) collective-permute-start(bf16[24,40,256]{2,1,0:T(8,128)(2,1)S(1)} %get-tuple-element.32), channel_id=1, source_target_pairs={{16,0},{17,1},{18,2},{19,3},{20,4},{21,5},{22,6},{23,7},{24,8},{25... | collective-permute-start | bytes 1474568 | tf_op jit(solution)/shard_map/ppermute | solution.py:160
  89.9 0.2 select_reduce_fusion
  90.1 0.1 pad_maximum_fusion
  90.2 0.4 convolution_bitcast_fusion.1
  90.6 8.9 %collective-permute-done.11 = bf16[24,40,256]{2,1,0:T(8,128)(2,1)S(1)} collective-permute-done((bf16[24,40,256]{2,1,0:T(8,128)(2,1)S(1)}, bf16[24,40,256]{2,1,0:T(8,128)(2,1)S(1)}, u32[]{:S(2)}, u32[]{:S(2)}) %collective-permute-start.11) | collective-permute-done | bytes 491552 | tf_op jit(solution)/shard_map/ppermute | solution.py:155
  99.6 3.9 %collective-permute-done.12 = bf16[24,40,256]{2,1,0:T(8,128)(2,1)S(1)} collective-permute-done((bf16[24,40,256]{2,1,0:T(8,128)(2,1)S(1)}, bf16[24,40,256]{2,1,0:T(8,128)(2,1)S(1)}, u32[]{:S(2)}, u32[]{:S(2)}) %collective-permute-start.12) | collective-permute-done | bytes 491552 | tf_op jit(solution)/shard_map/ppermute | solution.py:160
  103.5 0.1 pad_maximum_fusion.1
  103.6 1.5 %fusion.1 = f32[40,32,256]{2,1,0:T(8,128)} fusion(f32[40,32,256]{2,1,0:T(8,128)S(1)} %convolution_bitcast_fusion.1, bf16[48,40,256]{2,1,0:T(8,128)(2,1)S(1)} %pad_maximum_fusion.1, f32[32]{0:T(128)S(1)} %sqrt.4, bf16[24,32]{0,1:T(8,128)(2,1)S(1)} %get-tuple-element.39, bf16[24,32]{0,1:T(8,128)(2,1)S(1)} %get-tuple-element.37), kind=kOutput, calls=%fused_computation.2 | convolution fusion | flops 32118784 | bytes 3607680 | tf_op jit(solution)/shard_map/jmc,jr->mrc/dot_general | solution.py:265
  (28 shorter events, 0.5 us)
Async XLA Ops:
  0.0 17.1 %copy-start = (s32[32]{0:T(128)S(1)}, s32[32]{0:T(128)}, u32[]{:S(2)}) copy-start(s32[32]{0:T(128)} %constant.106.clone) | copy-start | bytes 388
  1.5 24.9 %collective-permute-start.4 = (bf16[32,40,256]{2,1,0:T(8,128)(2,1)S(1)}, bf16[32,40,256]{2,1,0:T(8,128)(2,1)S(1)}, u32[]{:S(2)}, u32[]{:S(2)}) collective-permute-start(bf16[32,40,256]{2,1,0:T(8,128)(2,1)S(1)} %bitcast.19), channel_id=1, source_target_pairs={{32,33},{33,34},{34,35},{35,36},{36,37},{37,38},{38,39},{39,40},{4... | collective-permute-start | bytes 1966088 | tf_op jit(solution)/shard_map/ppermute | solution.py:212
  2.2 19.4 %collective-permute-start.1 = (bf16[8,40,256]{2,1,0:T(8,128)(2,1)S(1)}, bf16[8,40,256]{2,1,0:T(8,128)(2,1)S(1)}, u32[]{:S(2)}, u32[]{:S(2)}) collective-permute-start(bf16[8,40,256]{2,1,0:T(8,128)(2,1)S(1)} %get-tuple-element.33), channel_id=1, source_target_pairs={{0,160},{1,161},{2,162},{3,163},{4,164},{5,165},{6,166},{7,167},{8... | collective-permute-start | bytes 491528 | tf_op jit(solution)/shard_map/ppermute | solution.py:206
  12.1 10.3 %collective-permute-start.3 = (bf16[8,40,256]{2,1,0:T(8,128)(2,1)S(1)}, bf16[8,40,256]{2,1,0:T(8,128)(2,1)S(1)}, u32[]{:S(2)}, u32[]{:S(2)}) collective-permute-start(bf16[8,40,256]{2,1,0:T(8,128)(2,1)S(1)} %get-tuple-element.34), channel_id=1, source_target_pairs={{0,288},{1,289},{2,290},{3,291},{4,292},{5,293},{6,294},{7,295},{8... | collective-permute-start | bytes 491528 | tf_op jit(solution)/shard_map/ppermute | solution.py:206
  14.4 8.7 %collective-permute-start.2 = (bf16[8,40,256]{2,1,0:T(8,128)(2,1)S(1)}, bf16[8,40,256]{2,1,0:T(8,128)(2,1)S(1)}, u32[]{:S(2)}, u32[]{:S(2)}) collective-permute-start(bf16[8,40,256]{2,1,0:T(8,128)(2,1)S(1)} %get-tuple-element.35), channel_id=1, source_target_pairs={{0,416},{1,417},{2,418},{3,419},{4,420},{5,421},{6,422},{7,423},{8... | collective-permute-start | bytes 491528 | tf_op jit(solution)/shard_map/ppermute | solution.py:206
  15.7 9.9 %collective-permute-start = (bf16[8,40,256]{2,1,0:T(8,128)(2,1)S(1)}, bf16[8,40,256]{2,1,0:T(8,128)(2,1)S(1)}, u32[]{:S(2)}, u32[]{:S(2)}) collective-permute-start(bf16[8,40,256]{2,1,0:T(8,128)(2,1)S(1)} %get-tuple-element.36), channel_id=1, source_target_pairs={{0,32},{1,33},{2,34},{3,35},{4,36},{5,37},{6,38},{7,39},{8,40},{9,... | collective-permute-start | bytes 491528 | tf_op jit(solution)/shard_map/ppermute | solution.py:206
  21.6 4.8 %collective-permute-start.5 = (bf16[32,40,256]{2,1,0:T(8,128)(2,1)S(1)}, bf16[32,40,256]{2,1,0:T(8,128)(2,1)S(1)}, u32[]{:S(2)}, u32[]{:S(2)}) collective-permute-start(bf16[32,40,256]{2,1,0:T(8,128)(2,1)S(1)} %bitcast.21), channel_id=1, source_target_pairs={{32,47},{33,32},{34,33},{35,34},{36,35},{37,36},{38,37},{39,38},{4... | collective-permute-start | bytes 1966088 | tf_op jit(solution)/shard_map/ppermute | solution.py:215
  27.4 59.7 %collective-permute-start.10 = (bf16[8,40,256]{2,1,0:T(8,128)(2,1)S(1)}, bf16[8,40,256]{2,1,0:T(8,128)(2,1)S(1)}, u32[]{:S(2)}, u32[]{:S(2)}) collective-permute-start(bf16[8,40,256]{2,1,0:T(8,128)(2,1)S(1)} %reshape.64), channel_id=1, source_target_pairs={{208,496},{209,497},{210,498},{211,499},{212,500},{213,501},{214,5... | collective-permute-start | bytes 491528 | tf_op jit(solution)/shard_map/ppermute | solution.py:233
  28.7 58.4 %collective-permute-start.9 = (bf16[8,40,256]{2,1,0:T(8,128)(2,1)S(1)}, bf16[8,40,256]{2,1,0:T(8,128)(2,1)S(1)}, u32[]{:S(2)}, u32[]{:S(2)}) collective-permute-start(bf16[8,40,256]{2,1,0:T(8,128)(2,1)S(1)} %reshape.64), channel_id=1, source_target_pairs={{80,496},{81,497},{82,498},{83,499},{84,500},{85,501},{86,502},{87... | collective-permute-start | bytes 491528 | tf_op jit(solution)/shard_map/ppermute | solution.py:233
  30.0 57.1 %collective-permute-start.8 = (bf16[8,40,256]{2,1,0:T(8,128)(2,1)S(1)}, bf16[8,40,256]{2,1,0:T(8,128)(2,1)S(1)}, u32[]{:S(2)}, u32[]{:S(2)}) collective-permute-start(bf16[8,40,256]{2,1,0:T(8,128)(2,1)S(1)} %reshape.64), channel_id=1, source_target_pairs={{144,16},{145,17},{146,18},{147,19},{148,20},{149,21},{150,22},{15... | collective-permute-start | bytes 491528 | tf_op jit(solution)/shard_map/ppermute | solution.py:233
  31.3 55.7 %collective-permute-start.7 = (bf16[8,40,256]{2,1,0:T(8,128)(2,1)S(1)}, bf16[8,40,256]{2,1,0:T(8,128)(2,1)S(1)}, u32[]{:S(2)}, u32[]{:S(2)}) collective-permute-start(bf16[8,40,256]{2,1,0:T(8,128)(2,1)S(1)} %reshape.64), channel_id=1, source_target_pairs={{32,0},{33,1},{34,2},{35,3},{36,4},{37,5},{38,6},{39,7},{40,8},{41... | collective-permute-start | bytes 491528 | tf_op jit(solution)/shard_map/ppermute | solution.py:233
  35.8 54.3 %collective-permute-start.6 = (bf16[24,40,256]{2,1,0:T(8,128)(2,1)S(1)}, bf16[24,40,256]{2,1,0:T(8,128)(2,1)S(1)}, u32[]{:S(2)}, u32[]{:S(2)}) collective-permute-start(bf16[24,40,256]{2,1,0:T(8,128)(2,1)S(1)} %slice_select_fusion), channel_id=1, source_target_pairs={{48,64},{49,65},{50,66},{51,67},{52,68},{53,69},{54,70},{55,71},{5... | collective-permute-start | bytes 1474568 | tf_op jit(solution)/shard_map/ppermute | solution.py:148
  87.3 12.3 %collective-permute-start.11 = (bf16[24,40,256]{2,1,0:T(8,128)(2,1)S(1)}, bf16[24,40,256]{2,1,0:T(8,128)(2,1)S(1)}, u32[]{:S(2)}, u32[]{:S(2)}) collective-permute-start(bf16[24,40,256]{2,1,0:T(8,128)(2,1)S(1)} %get-tuple-element.31), channel_id=1, source_target_pairs={{0,16},{1,17},{2,18},{3,19},{4,20},{5,21},{6,22},{7,23},{8,24},{9,... | collective-permute-start | bytes 1474568 | tf_op jit(solution)/shard_map/ppermute | solution.py:155
  88.6 14.9 %collective-permute-start.12 = (bf16[24,40,256]{2,1,0:T(8,128)(2,1)S(1)}, bf16[24,40,256]{2,1,0:T(8,128)(2,1)S(1)}, u32[]{:S(2)}, u32[]{:S(2)}) collective-permute-start(bf16[24,40,256]{2,1,0:T(8,128)(2,1)S(1)} %get-tuple-element.32), channel_id=1, source_target_pairs={{16,0},{17,1},{18,2},{19,3},{20,4},{21,5},{22,6},{23,7},{24,8},{25... | collective-permute-start | bytes 1474568 | tf_op jit(solution)/shard_map/ppermute | solution.py:160

commit v5 on v4

--- a/solution.py
+++ b/solution.py
@@ -72,6 +72,7 @@
 
 def circle_kernel(width_ref, level_ref, data_ref, out_ref, tiles, twice, total):
     blocks, members, cols = data_ref.shape
+    members, cols = members // 2, cols * 2
     span = twice.shape[0] // (2 * blocks)
     size = blocks * span
     count = blocks * cols // TILE
@@ -89,7 +90,9 @@
             tiles[count - n] = tile.T
     pad = jnp.zeros((span - members, cols), jnp.bfloat16)
     for i in range(blocks):
-        block = jnp.concatenate([data_ref[i], pad], axis=0)
+        halves = data_ref[i]
+        block = jnp.concatenate([halves[:members], halves[members:]], axis=1)
+        block = jnp.concatenate([block, pad], axis=0)
         twice[i * span : (i + 1) * span] = block
         twice[size + i * span : size + (i + 1) * span] = block
     for k in range(blocks):
@@ -106,11 +109,13 @@
         else:
             total[...] += part
     for i in range(blocks):
-        out_ref[i] = total[i * span : i * span + members].astype(jnp.bfloat16)
+        block = total[i * span : i * span + members].astype(jnp.bfloat16)
+        out_ref[i] = jnp.concatenate([block[:, : cols // 2], block[:, cols // 2 :]], axis=0)
 
 
 def unit_product(parts, width, level):
     blocks, members, cols = parts.shape
+    members, cols = members // 2, cols * 2
     span = members + -members % 16
     smem = pl.BlockSpec(memory_space=pltpu.SMEM)
     vmem = pl.BlockSpec(memory_space=pltpu.VMEM)
@@ -207,7 +212,9 @@
     ]
     handed[1], late = lax.optimization_barrier((handed[1], data))
     given = jnp.where(keeps, data[:share], sum(handed))
-    parts = given.reshape(lon_count, member_count // pieces, lon_cols)
+    group = member_count // pieces
+    parts = given.reshape(share, pieces, group, 2, lon_cols // 2).transpose(0, 1, 3, 2, 4)
+    parts = parts.reshape(lon_count, 2 * group, lon_cols // 2)
 
     left = lax.ppermute(
         data, axes, pairs(lambda lat, lon: None if polar_of(lat) else (lat, lon + 1))
@@ -229,7 +236,8 @@
     near = near_product(left, data, right, widths, levels)
 
     far = far_halo(near, lat_index, lat_count, lon_count)
-    done = parts.reshape(share, member_count, lon_cols)
+    done = parts.reshape(share, pieces, 2, group, lon_cols // 2).transpose(0, 1, 3, 2, 4)
+    done = done.reshape(share, member_count, lon_cols)
     polar = [lax.ppermute(done, axes, pairs(returns(q))) for q in range(shares)]
     polar[0] = jnp.where(keeps, done, polar[0])
     polar = jnp.concatenate(polar, axis=0)

time: 106 us -> 102 us (0.962)
  waiting for transfers between devices: 66.6 us -> 63.9 us
  local copies, waits for them, and re-layouts: 5.2 us -> 4.04 us
    ppermute x4, waiting for transfers between devices: 50.5 us -> 48.4 us  [body(): polar = [lax.ppermute(done, axes, pairs(returns(q))) for q in range(shares)]]
    reshape x2 -> x4, local copies, waits for them, and re-layouts: 1.68 us -> 0.33 us  [the longest x2 0.17 us: body(): given.reshape(share, pieces, group, 2, lon_cols // 2)]
  transfers between devices with their start and end apart: 13 -> 13, of which waited for: 5 -> 5; matrix products, arithmetic and copies ran while one was open for 5% -> 4% of each run, Pallas kernels for 3% -> 3%
where the time goes in v5:
time: 102 us; the launch traced here: 101 us
  waiting for transfers between devices  63.9 us (63%)
  starting transfers between devices  24.7 us (24%)
  local copies, waits for them, and re-layouts  4.04 us (4%)
  Pallas kernels  3.18 us (3%)
  other arithmetic  1.93 us (2%)
  matrix products  1.88 us (2%)
  between operations  1.69 us (2%)
    ppermute x4, waiting for transfers between devices, body(): polar = [lax.ppermute(done, axes, pairs(returns(q))) for q in range(shares)]  48.4 us
    ppermute x4, starting transfers between devices, body(): lax.ppermute(data[q * share:(q + 1) * share], axes, pairs(hands(q)))  14.8 us
    ppermute x1, waiting for transfers between devices, next_halo(): lax.ppermute(along[-HALF_LAT:], axes, pairs(lambda lat, lon: (lat + 1, lo...  8.46 us
    ppermute x4, starting transfers between devices, body(): polar = [lax.ppermute(done, axes, pairs(returns(q))) for q in range(shares)]  5.17 us
    ppermute x1, waiting for transfers between devices, next_halo(): lax.ppermute(along[:HALF_LAT], axes, pairs(lambda lat, lon: (lat - 1, lon...  3.82 us
    pallas_call x1, Pallas kernels, near_product(): pl.pallas_call(near_kernel, grid=(rows // step,), in_specs=[smem, smem, b...  3.18 us
    ppermute x4, waiting for transfers between devices, body(): lax.ppermute(data[q * share:(q + 1) * share], axes, pairs(hands(q)))  3.17 us
  transfers between devices with their start and end apart: 13, of which 5 were waited for; matrix products, arithmetic and copies ran while one was open for 4% of the time, Pallas kernels for 3%

profile of v5, /device:TPU:1, one launch (start us, length us, event | category | flops | bytes accessed | tf_op | source)
XLA Modules:
  0.0 101.3 jit_solution(3731451480833913848)
XLA Ops:
  0.0 1.5 %copy.31 = bf16[40,32,256]{2,0,1:T(8,128)(2,1)S(1)} copy(bf16[40,32,256]{2,1,0:T(8,128)(2,1)} %param.5) | data formatting | bytes 1310720 | tf_op args[0]
  1.5 0.7 collective-permute-start.4
  2.2 9.9 %collective-permute-start.1 = (bf16[8,40,256]{2,1,0:T(8,128)(2,1)S(1)}, bf16[8,40,256]{2,1,0:T(8,128)(2,1)S(1)}, u32[]{:S(2)}, u32[]{:S(2)}) collective-permute-start(bf16[8,40,256]{2,1,0:T(8,128)(2,1)S(1)} %get-tuple-element.41), channel_id=1, source_target_pairs={{0,160},{1,161},{2,162},{3,163},{4,164},{5,165},{6,166},{7,167},{8... | collective-permute-start | bytes 491528 | tf_op jit(solution)/shard_map/ppermute | solution.py:211
  12.1 2.3 %collective-permute-start.3 = (bf16[8,40,256]{2,1,0:T(8,128)(2,1)S(1)}, bf16[8,40,256]{2,1,0:T(8,128)(2,1)S(1)}, u32[]{:S(2)}, u32[]{:S(2)}) collective-permute-start(bf16[8,40,256]{2,1,0:T(8,128)(2,1)S(1)} %get-tuple-element.42), channel_id=1, source_target_pairs={{0,288},{1,289},{2,290},{3,291},{4,292},{5,293},{6,294},{7,295},{8... | collective-permute-start | bytes 491528 | tf_op jit(solution)/shard_map/ppermute | solution.py:211
  14.4 1.3 %collective-permute-start.2 = (bf16[8,40,256]{2,1,0:T(8,128)(2,1)S(1)}, bf16[8,40,256]{2,1,0:T(8,128)(2,1)S(1)}, u32[]{:S(2)}, u32[]{:S(2)}) collective-permute-start(bf16[8,40,256]{2,1,0:T(8,128)(2,1)S(1)} %get-tuple-element.43), channel_id=1, source_target_pairs={{0,416},{1,417},{2,418},{3,419},{4,420},{5,421},{6,422},{7,423},{8... | collective-permute-start | bytes 491528 | tf_op jit(solution)/shard_map/ppermute | solution.py:211
  15.7 1.3 %collective-permute-start = (bf16[8,40,256]{2,1,0:T(8,128)(2,1)S(1)}, bf16[8,40,256]{2,1,0:T(8,128)(2,1)S(1)}, u32[]{:S(2)}, u32[]{:S(2)}) collective-permute-start(bf16[8,40,256]{2,1,0:T(8,128)(2,1)S(1)} %get-tuple-element.44), channel_id=1, source_target_pairs={{0,32},{1,33},{2,34},{3,35},{4,36},{5,37},{6,38},{7,39},{8,40},{9,... | collective-permute-start | bytes 491528 | tf_op jit(solution)/shard_map/ppermute | solution.py:211
  17.1 0.6 dynamic_slice.10
  18.4 0.8 dynamic-slice_convert_fusion.width_ref
  19.2 1.3 %dynamic_slice.11 = s32[1]{0:T(128)} dynamic-slice(s32[1024]{0:T(1024)} %param.6, s32[]{:T(128)S(6)} %select_n.86), dynamic_slice_sizes={1} | dynamic-slice | bytes 12 | tf_op jit(solution)/shard_map/dynamic_slice | solution.py:226
  21.3 0.3 fusion.6
  21.6 0.7 collective-permute-start.5
  22.5 0.7 collective-permute-done.2
  23.2 2.5 %collective-permute-done = bf16[8,40,256]{2,1,0:T(8,128)(2,1)S(1)} collective-permute-done((bf16[8,40,256]{2,1,0:T(8,128)(2,1)S(1)}, bf16[8,40,256]{2,1,0:T(8,128)(2,1)S(1)}, u32[]{:S(2)}, u32[]{:S(2)}) %collective-permute-start) | collective-permute-done | bytes 163872 | tf_op jit(solution)/shard_map/ppermute | solution.py:211
  25.7 0.1 copy.18
  26.0 0.2 copy.22
  26.2 0.1 reshape.72
  26.3 1.3 %collective-permute-start.10 = (bf16[8,40,256]{2,1,0:T(8,128)(2,1)S(1)}, bf16[8,40,256]{2,1,0:T(8,128)(2,1)S(1)}, u32[]{:S(2)}, u32[]{:S(2)}) collective-permute-start(bf16[8,40,256]{2,1,0:T(8,128)(2,1)S(1)} %reshape.72), channel_id=1, source_target_pairs={{208,496},{209,497},{210,498},{211,499},{212,500},{213,501},{214,5... | collective-permute-start | bytes 491528 | tf_op jit(solution)/shard_map/ppermute | solution.py:241
  27.6 1.3 %collective-permute-start.9 = (bf16[8,40,256]{2,1,0:T(8,128)(2,1)S(1)}, bf16[8,40,256]{2,1,0:T(8,128)(2,1)S(1)}, u32[]{:S(2)}, u32[]{:S(2)}) collective-permute-start(bf16[8,40,256]{2,1,0:T(8,128)(2,1)S(1)} %reshape.72), channel_id=1, source_target_pairs={{80,496},{81,497},{82,498},{83,499},{84,500},{85,501},{86,502},{87... | collective-permute-start | bytes 491528 | tf_op jit(solution)/shard_map/ppermute | solution.py:241
  28.9 1.3 %collective-permute-start.8 = (bf16[8,40,256]{2,1,0:T(8,128)(2,1)S(1)}, bf16[8,40,256]{2,1,0:T(8,128)(2,1)S(1)}, u32[]{:S(2)}, u32[]{:S(2)}) collective-permute-start(bf16[8,40,256]{2,1,0:T(8,128)(2,1)S(1)} %reshape.72), channel_id=1, source_target_pairs={{144,16},{145,17},{146,18},{147,19},{148,20},{149,21},{150,22},{15... | collective-permute-start | bytes 491528 | tf_op jit(solution)/shard_map/ppermute | solution.py:241
  30.2 1.3 %collective-permute-start.7 = (bf16[8,40,256]{2,1,0:T(8,128)(2,1)S(1)}, bf16[8,40,256]{2,1,0:T(8,128)(2,1)S(1)}, u32[]{:S(2)}, u32[]{:S(2)}) collective-permute-start(bf16[8,40,256]{2,1,0:T(8,128)(2,1)S(1)} %reshape.72), channel_id=1, source_target_pairs={{32,0},{33,1},{34,2},{35,3},{36,4},{37,5},{38,6},{39,7},{40,8},{41... | collective-permute-start | bytes 491528 | tf_op jit(solution)/shard_map/ppermute | solution.py:241
  31.5 3.2 %shard_map.37 = bf16[32,40,256]{2,1,0:T(8,128)(2,1)S(1)} custom-call(f32[32]{0:T(128)S(1)} %dynamic-slice_convert_fusion.width_ref, f32[32]{0:T(128)S(1)} %bitcast.33, bf16[32,40,256]{2,1,0:T(8,128)(2,1)S(1)} %collective-permute-done.4.left_ref, bf16[32,40,256]{2,1,0:T(8,128)(2,1)S(1)} %bitcast.29, bf16[32,40,256]{2,1,0:T(8,128)(2,1)S(1)} %collective-permute-done.5.right_ref), custom_call_target="tpu_custom_call" | custom-call | tf_op jit(solution)/shard_map/pallas_call | solution.py:63
  34.7 0.7 collective-permute-start.6
  35.4 48.4 %collective-permute-done.7 = bf16[8,40,256]{2,1,0:T(8,128)(2,1)S(1)} collective-permute-done((bf16[8,40,256]{2,1,0:T(8,128)(2,1)S(1)}, bf16[8,40,256]{2,1,0:T(8,128)(2,1)S(1)}, u32[]{:S(2)}, u32[]{:S(2)}) %collective-permute-start.7) | collective-permute-done | bytes 163872 | tf_op jit(solution)/shard_map/ppermute | solution.py:241
  83.8 0.1 maximum_select_fusion
  84.1 1.3 %collective-permute-start.11 = (bf16[24,40,256]{2,1,0:T(8,128)(2,1)S(1)}, bf16[24,40,256]{2,1,0:T(8,128)(2,1)S(1)}, u32[]{:S(2)}, u32[]{:S(2)}) collective-permute-start(bf16[24,40,256]{2,1,0:T(8,128)(2,1)S(1)} %get-tuple-element.39), channel_id=1, source_target_pairs={{0,16},{1,17},{2,18},{3,19},{4,20},{5,21},{6,22},{7,23},{8,24},{9,... | collective-permute-start | bytes 1474568 | tf_op jit(solution)/shard_map/ppermute | solution.py:160
  85.4 1.3 %collective-permute-start.12 = (bf16[24,40,256]{2,1,0:T(8,128)(2,1)S(1)}, bf16[24,40,256]{2,1,0:T(8,128)(2,1)S(1)}, u32[]{:S(2)}, u32[]{:S(2)}) collective-permute-start(bf16[24,40,256]{2,1,0:T(8,128)(2,1)S(1)} %get-tuple-element.40), channel_id=1, source_target_pairs={{16,0},{17,1},{18,2},{19,3},{20,4},{21,5},{22,6},{23,7},{24,8},{25... | collective-permute-start | bytes 1474568 | tf_op jit(solution)/shard_map/ppermute | solution.py:165
  86.7 0.2 select_reduce_fusion
  86.9 0.1 pad_maximum_fusion
  87.0 0.4 convolution_bitcast_fusion.1
  87.4 8.5 %collective-permute-done.11 = bf16[24,40,256]{2,1,0:T(8,128)(2,1)S(1)} collective-permute-done((bf16[24,40,256]{2,1,0:T(8,128)(2,1)S(1)}, bf16[24,40,256]{2,1,0:T(8,128)(2,1)S(1)}, u32[]{:S(2)}, u32[]{:S(2)}) %collective-permute-start.11) | collective-permute-done | bytes 491552 | tf_op jit(solution)/shard_map/ppermute | solution.py:160
  95.9 3.8 %collective-permute-done.12 = bf16[24,40,256]{2,1,0:T(8,128)(2,1)S(1)} collective-permute-done((bf16[24,40,256]{2,1,0:T(8,128)(2,1)S(1)}, bf16[24,40,256]{2,1,0:T(8,128)(2,1)S(1)}, u32[]{:S(2)}, u32[]{:S(2)}) %collective-permute-start.12) | collective-permute-done | bytes 491552 | tf_op jit(solution)/shard_map/ppermute | solution.py:165
  99.8 1.5 %fusion.1 = f32[40,32,256]{2,1,0:T(8,128)} fusion(f32[40,32,256]{2,1,0:T(8,128)S(1)} %convolution_bitcast_fusion.1, bf16[48,40,256]{2,1,0:T(8,128)(2,1)S(1)} %pad_maximum_fusion.1, f32[32]{0:T(128)S(1)} %sqrt.4, bf16[24,32]{0,1:T(8,128)(2,1)S(1)} %get-tuple-element.47, bf16[24,32]{0,1:T(8,128)(2,1)S(1)} %get-tuple-element.45), kind=kOutput, calls=%fused_computation.2 | convolution fusion | flops 32118784 | bytes 3607680 | tf_op jit(solution)/shard_map/jmc,jr->mrc/dot_general | solution.py:273
  (32 shorter events, 0.8 us)
Async XLA Ops:
  0.0 17.1 %copy-start = (s32[32]{0:T(128)S(1)}, s32[32]{0:T(128)}, u32[]{:S(2)}) copy-start(s32[32]{0:T(128)} %constant.106.clone) | copy-start | bytes 388
  1.5 24.5 %collective-permute-start.4 = (bf16[32,40,256]{2,1,0:T(8,128)(2,1)S(1)}, bf16[32,40,256]{2,1,0:T(8,128)(2,1)S(1)}, u32[]{:S(2)}, u32[]{:S(2)}) collective-permute-start(bf16[32,40,256]{2,1,0:T(8,128)(2,1)S(1)} %bitcast.25), channel_id=1, source_target_pairs={{32,33},{33,34},{34,35},{35,36},{36,37},{37,38},{38,39},{39,40},{4... | collective-permute-start | bytes 1966088 | tf_op jit(solution)/shard_map/ppermute | solution.py:219
  2.2 19.4 %collective-permute-start.1 = (bf16[8,40,256]{2,1,0:T(8,128)(2,1)S(1)}, bf16[8,40,256]{2,1,0:T(8,128)(2,1)S(1)}, u32[]{:S(2)}, u32[]{:S(2)}) collective-permute-start(bf16[8,40,256]{2,1,0:T(8,128)(2,1)S(1)} %get-tuple-element.41), channel_id=1, source_target_pairs={{0,160},{1,161},{2,162},{3,163},{4,164},{5,165},{6,166},{7,167},{8... | collective-permute-start | bytes 491528 | tf_op jit(solution)/shard_map/ppermute | solution.py:211
  12.1 10.3 %collective-permute-start.3 = (bf16[8,40,256]{2,1,0:T(8,128)(2,1)S(1)}, bf16[8,40,256]{2,1,0:T(8,128)(2,1)S(1)}, u32[]{:S(2)}, u32[]{:S(2)}) collective-permute-start(bf16[8,40,256]{2,1,0:T(8,128)(2,1)S(1)} %get-tuple-element.42), channel_id=1, source_target_pairs={{0,288},{1,289},{2,290},{3,291},{4,292},{5,293},{6,294},{7,295},{8... | collective-permute-start | bytes 491528 | tf_op jit(solution)/shard_map/ppermute | solution.py:211
  14.4 8.7 %collective-permute-start.2 = (bf16[8,40,256]{2,1,0:T(8,128)(2,1)S(1)}, bf16[8,40,256]{2,1,0:T(8,128)(2,1)S(1)}, u32[]{:S(2)}, u32[]{:S(2)}) collective-permute-start(bf16[8,40,256]{2,1,0:T(8,128)(2,1)S(1)} %get-tuple-element.43), channel_id=1, source_target_pairs={{0,416},{1,417},{2,418},{3,419},{4,420},{5,421},{6,422},{7,423},{8... | collective-permute-start | bytes 491528 | tf_op jit(solution)/shard_map/ppermute | solution.py:211
  15.7 9.9 %collective-permute-start = (bf16[8,40,256]{2,1,0:T(8,128)(2,1)S(1)}, bf16[8,40,256]{2,1,0:T(8,128)(2,1)S(1)}, u32[]{:S(2)}, u32[]{:S(2)}) collective-permute-start(bf16[8,40,256]{2,1,0:T(8,128)(2,1)S(1)} %get-tuple-element.44), channel_id=1, source_target_pairs={{0,32},{1,33},{2,34},{3,35},{4,36},{5,37},{6,38},{7,39},{8,40},{9,... | collective-permute-start | bytes 491528 | tf_op jit(solution)/shard_map/ppermute | solution.py:211
  21.6 4.3 %collective-permute-start.5 = (bf16[32,40,256]{2,1,0:T(8,128)(2,1)S(1)}, bf16[32,40,256]{2,1,0:T(8,128)(2,1)S(1)}, u32[]{:S(2)}, u32[]{:S(2)}) collective-permute-start(bf16[32,40,256]{2,1,0:T(8,128)(2,1)S(1)} %bitcast.27), channel_id=1, source_target_pairs={{32,47},{33,32},{34,33},{35,34},{36,35},{37,36},{38,37},{39,38},{4... | collective-permute-start | bytes 1966088 | tf_op jit(solution)/shard_map/ppermute | solution.py:222
  26.3 57.5 %collective-permute-start.10 = (bf16[8,40,256]{2,1,0:T(8,128)(2,1)S(1)}, bf16[8,40,256]{2,1,0:T(8,128)(2,1)S(1)}, u32[]{:S(2)}, u32[]{:S(2)}) collective-permute-start(bf16[8,40,256]{2,1,0:T(8,128)(2,1)S(1)} %reshape.72), channel_id=1, source_target_pairs={{208,496},{209,497},{210,498},{211,499},{212,500},{213,501},{214,5... | collective-permute-start | bytes 491528 | tf_op jit(solution)/shard_map/ppermute | solution.py:241
  27.6 56.3 %collective-permute-start.9 = (bf16[8,40,256]{2,1,0:T(8,128)(2,1)S(1)}, bf16[8,40,256]{2,1,0:T(8,128)(2,1)S(1)}, u32[]{:S(2)}, u32[]{:S(2)}) collective-permute-start(bf16[8,40,256]{2,1,0:T(8,128)(2,1)S(1)} %reshape.72), channel_id=1, source_target_pairs={{80,496},{81,497},{82,498},{83,499},{84,500},{85,501},{86,502},{87... | collective-permute-start | bytes 491528 | tf_op jit(solution)/shard_map/ppermute | solution.py:241
  28.9 55.0 %collective-permute-start.8 = (bf16[8,40,256]{2,1,0:T(8,128)(2,1)S(1)}, bf16[8,40,256]{2,1,0:T(8,128)(2,1)S(1)}, u32[]{:S(2)}, u32[]{:S(2)}) collective-permute-start(bf16[8,40,256]{2,1,0:T(8,128)(2,1)S(1)} %reshape.72), channel_id=1, source_target_pairs={{144,16},{145,17},{146,18},{147,19},{148,20},{149,21},{150,22},{15... | collective-permute-start | bytes 491528 | tf_op jit(solution)/shard_map/ppermute | solution.py:241
  30.2 53.6 %collective-permute-start.7 = (bf16[8,40,256]{2,1,0:T(8,128)(2,1)S(1)}, bf16[8,40,256]{2,1,0:T(8,128)(2,1)S(1)}, u32[]{:S(2)}, u32[]{:S(2)}) collective-permute-start(bf16[8,40,256]{2,1,0:T(8,128)(2,1)S(1)} %reshape.72), channel_id=1, source_target_pairs={{32,0},{33,1},{34,2},{35,3},{36,4},{37,5},{38,6},{39,7},{40,8},{41... | collective-permute-start | bytes 491528 | tf_op jit(solution)/shard_map/ppermute | solution.py:241
  34.7 52.2 %collective-permute-start.6 = (bf16[24,40,256]{2,1,0:T(8,128)(2,1)S(1)}, bf16[24,40,256]{2,1,0:T(8,128)(2,1)S(1)}, u32[]{:S(2)}, u32[]{:S(2)}) collective-permute-start(bf16[24,40,256]{2,1,0:T(8,128)(2,1)S(1)} %slice_select_fusion), channel_id=1, source_target_pairs={{48,64},{49,65},{50,66},{51,67},{52,68},{53,69},{54,70},{55,71},{5... | collective-permute-start | bytes 1474568 | tf_op jit(solution)/shard_map/ppermute | solution.py:153
  84.1 11.8 %collective-permute-start.11 = (bf16[24,40,256]{2,1,0:T(8,128)(2,1)S(1)}, bf16[24,40,256]{2,1,0:T(8,128)(2,1)S(1)}, u32[]{:S(2)}, u32[]{:S(2)}) collective-permute-start(bf16[24,40,256]{2,1,0:T(8,128)(2,1)S(1)} %get-tuple-element.39), channel_id=1, source_target_pairs={{0,16},{1,17},{2,18},{3,19},{4,20},{5,21},{6,22},{7,23},{8,24},{9,... | collective-permute-start | bytes 1474568 | tf_op jit(solution)/shard_map/ppermute | solution.py:160
  85.4 14.3 %collective-permute-start.12 = (bf16[24,40,256]{2,1,0:T(8,128)(2,1)S(1)}, bf16[24,40,256]{2,1,0:T(8,128)(2,1)S(1)}, u32[]{:S(2)}, u32[]{:S(2)}) collective-permute-start(bf16[24,40,256]{2,1,0:T(8,128)(2,1)S(1)} %get-tuple-element.40), channel_id=1, source_target_pairs={{16,0},{17,1},{18,2},{19,3},{20,4},{21,5},{22,6},{23,7},{24,8},{25... | collective-permute-start | bytes 1474568 | tf_op jit(solution)/shard_map/ppermute | solution.py:165

commit v6 on v5

--- a/solution.py
+++ b/solution.py
@@ -95,16 +95,17 @@
         block = jnp.concatenate([block, pad], axis=0)
         twice[i * span : (i + 1) * span] = block
         twice[size + i * span : size + (i + 1) * span] = block
-    for k in range(blocks):
-        weights = jnp.concatenate(
-            [
-                jnp.concatenate([tiles[2 * k], tiles[(2 * k - 1) % count]], axis=1),
-                jnp.concatenate([tiles[(2 * k + 1) % count], tiles[2 * k]], axis=1),
-            ],
-            axis=0,
-        )
-        part = jnp.dot(twice[k * span : k * span + size], weights, preferred_element_type=jnp.float32)
-        if k == 0:
+    step = 4
+    for first in range(0, blocks, step):
+        steps = range(first, first + step)
+        weights = [
+            jnp.concatenate([tiles[(2 * k + half) % count], tiles[(2 * k + half - 1) % count]], axis=1)
+            for k in steps
+            for half in range(2)
+        ]
+        data = jnp.concatenate([twice[k * span : k * span + size] for k in steps], axis=1)
+        part = jnp.dot(data, jnp.concatenate(weights, axis=0), preferred_element_type=jnp.float32)
+        if first == 0:
             total[...] = part
         else:
             total[...] += part

time: 102 us -> 102 us (level)
  no operation moved by 1% of the time
where the time goes in v6:
time: 102 us; the launch traced here: 101 us
  waiting for transfers between devices  63.8 us (63%)
  starting transfers between devices  24.7 us (24%)
  local copies, waits for them, and re-layouts  4.04 us (4%)
  Pallas kernels  3.18 us (3%)
  other arithmetic  1.93 us (2%)
  matrix products  1.88 us (2%)
  between operations  1.69 us (2%)
    ppermute x4, waiting for transfers between devices, body(): polar = [lax.ppermute(done, axes, pairs(returns(q))) for q in range(shares)]  48.4 us
    ppermute x4, starting transfers between devices, body(): lax.ppermute(data[q * share:(q + 1) * share], axes, pairs(hands(q)))  14.8 us
    ppermute x1, waiting for transfers between devices, next_halo(): lax.ppermute(along[-HALF_LAT:], axes, pairs(lambda lat, lon: (lat + 1, lo...  8.46 us
    ppermute x4, starting transfers between devices, body(): polar = [lax.ppermute(done, axes, pairs(returns(q))) for q in range(shares)]  5.17 us
    ppermute x1, waiting for transfers between devices, next_halo(): lax.ppermute(along[:HALF_LAT], axes, pairs(lambda lat, lon: (lat - 1, lon...  3.82 us
    pallas_call x1, Pallas kernels, near_product(): pl.pallas_call(near_kernel, grid=(rows // step,), in_specs=[smem, smem, b...  3.18 us
    ppermute x4, waiting for transfers between devices, body(): lax.ppermute(data[q * share:(q + 1) * share], axes, pairs(hands(q)))  3.17 us
  transfers between devices with their start and end apart: 13, of which 5 were waited for; matrix products, arithmetic and copies ran while one was open for 4% of the time, Pallas kernels for 3%

profile of v6, /device:TPU:1, one launch (start us, length us, event | category | flops | bytes accessed | tf_op | source)
XLA Modules:
  0.0 101.3 jit_solution(11668587649283269742)
XLA Ops:
  0.0 1.5 %copy.31 = bf16[40,32,256]{2,0,1:T(8,128)(2,1)S(1)} copy(bf16[40,32,256]{2,1,0:T(8,128)(2,1)} %param.5) | data formatting | bytes 1310720 | tf_op args[0]
  1.5 0.7 collective-permute-start.4
  2.2 9.9 %collective-permute-start.1 = (bf16[8,40,256]{2,1,0:T(8,128)(2,1)S(1)}, bf16[8,40,256]{2,1,0:T(8,128)(2,1)S(1)}, u32[]{:S(2)}, u32[]{:S(2)}) collective-permute-start(bf16[8,40,256]{2,1,0:T(8,128)(2,1)S(1)} %get-tuple-element.41), channel_id=1, source_target_pairs={{0,160},{1,161},{2,162},{3,163},{4,164},{5,165},{6,166},{7,167},{8... | collective-permute-start | bytes 491528 | tf_op jit(solution)/shard_map/ppermute | solution.py:212
  12.1 2.3 %collective-permute-start.3 = (bf16[8,40,256]{2,1,0:T(8,128)(2,1)S(1)}, bf16[8,40,256]{2,1,0:T(8,128)(2,1)S(1)}, u32[]{:S(2)}, u32[]{:S(2)}) collective-permute-start(bf16[8,40,256]{2,1,0:T(8,128)(2,1)S(1)} %get-tuple-element.42), channel_id=1, source_target_pairs={{0,288},{1,289},{2,290},{3,291},{4,292},{5,293},{6,294},{7,295},{8... | collective-permute-start | bytes 491528 | tf_op jit(solution)/shard_map/ppermute | solution.py:212
  14.4 1.3 %collective-permute-start.2 = (bf16[8,40,256]{2,1,0:T(8,128)(2,1)S(1)}, bf16[8,40,256]{2,1,0:T(8,128)(2,1)S(1)}, u32[]{:S(2)}, u32[]{:S(2)}) collective-permute-start(bf16[8,40,256]{2,1,0:T(8,128)(2,1)S(1)} %get-tuple-element.43), channel_id=1, source_target_pairs={{0,416},{1,417},{2,418},{3,419},{4,420},{5,421},{6,422},{7,423},{8... | collective-permute-start | bytes 491528 | tf_op jit(solution)/shard_map/ppermute | solution.py:212
  15.7 1.3 %collective-permute-start = (bf16[8,40,256]{2,1,0:T(8,128)(2,1)S(1)}, bf16[8,40,256]{2,1,0:T(8,128)(2,1)S(1)}, u32[]{:S(2)}, u32[]{:S(2)}) collective-permute-start(bf16[8,40,256]{2,1,0:T(8,128)(2,1)S(1)} %get-tuple-element.44), channel_id=1, source_target_pairs={{0,32},{1,33},{2,34},{3,35},{4,36},{5,37},{6,38},{7,39},{8,40},{9,... | collective-permute-start | bytes 491528 | tf_op jit(solution)/shard_map/ppermute | solution.py:212
  17.1 0.6 dynamic_slice.10
  18.4 0.8 dynamic-slice_convert_fusion.width_ref
  19.2 1.3 %dynamic_slice.11 = s32[1]{0:T(128)} dynamic-slice(s32[1024]{0:T(1024)} %param.6, s32[]{:T(128)S(6)} %select_n.86), dynamic_slice_sizes={1} | dynamic-slice | bytes 12 | tf_op jit(solution)/shard_map/dynamic_slice | solution.py:227
  21.3 0.3 fusion.6
  21.6 0.7 collective-permute-start.5
  22.5 0.7 collective-permute-done.2
  23.2 2.5 %collective-permute-done = bf16[8,40,256]{2,1,0:T(8,128)(2,1)S(1)} collective-permute-done((bf16[8,40,256]{2,1,0:T(8,128)(2,1)S(1)}, bf16[8,40,256]{2,1,0:T(8,128)(2,1)S(1)}, u32[]{:S(2)}, u32[]{:S(2)}) %collective-permute-start) | collective-permute-done | bytes 163872 | tf_op jit(solution)/shard_map/ppermute | solution.py:212
  25.7 0.1 copy.18
  26.0 0.2 copy.22
  26.2 0.1 reshape.72
  26.3 1.3 %collective-permute-start.10 = (bf16[8,40,256]{2,1,0:T(8,128)(2,1)S(1)}, bf16[8,40,256]{2,1,0:T(8,128)(2,1)S(1)}, u32[]{:S(2)}, u32[]{:S(2)}) collective-permute-start(bf16[8,40,256]{2,1,0:T(8,128)(2,1)S(1)} %reshape.72), channel_id=1, source_target_pairs={{208,496},{209,497},{210,498},{211,499},{212,500},{213,501},{214,5... | collective-permute-start | bytes 491528 | tf_op jit(solution)/shard_map/ppermute | solution.py:242
  27.6 1.3 %collective-permute-start.9 = (bf16[8,40,256]{2,1,0:T(8,128)(2,1)S(1)}, bf16[8,40,256]{2,1,0:T(8,128)(2,1)S(1)}, u32[]{:S(2)}, u32[]{:S(2)}) collective-permute-start(bf16[8,40,256]{2,1,0:T(8,128)(2,1)S(1)} %reshape.72), channel_id=1, source_target_pairs={{80,496},{81,497},{82,498},{83,499},{84,500},{85,501},{86,502},{87... | collective-permute-start | bytes 491528 | tf_op jit(solution)/shard_map/ppermute | solution.py:242
  28.9 1.3 %collective-permute-start.8 = (bf16[8,40,256]{2,1,0:T(8,128)(2,1)S(1)}, bf16[8,40,256]{2,1,0:T(8,128)(2,1)S(1)}, u32[]{:S(2)}, u32[]{:S(2)}) collective-permute-start(bf16[8,40,256]{2,1,0:T(8,128)(2,1)S(1)} %reshape.72), channel_id=1, source_target_pairs={{144,16},{145,17},{146,18},{147,19},{148,20},{149,21},{150,22},{15... | collective-permute-start | bytes 491528 | tf_op jit(solution)/shard_map/ppermute | solution.py:242
  30.2 1.3 %collective-permute-start.7 = (bf16[8,40,256]{2,1,0:T(8,128)(2,1)S(1)}, bf16[8,40,256]{2,1,0:T(8,128)(2,1)S(1)}, u32[]{:S(2)}, u32[]{:S(2)}) collective-permute-start(bf16[8,40,256]{2,1,0:T(8,128)(2,1)S(1)} %reshape.72), channel_id=1, source_target_pairs={{32,0},{33,1},{34,2},{35,3},{36,4},{37,5},{38,6},{39,7},{40,8},{41... | collective-permute-start | bytes 491528 | tf_op jit(solution)/shard_map/ppermute | solution.py:242
  31.5 3.2 %shard_map.37 = bf16[32,40,256]{2,1,0:T(8,128)(2,1)S(1)} custom-call(f32[32]{0:T(128)S(1)} %dynamic-slice_convert_fusion.width_ref, f32[32]{0:T(128)S(1)} %bitcast.33, bf16[32,40,256]{2,1,0:T(8,128)(2,1)S(1)} %collective-permute-done.4.left_ref, bf16[32,40,256]{2,1,0:T(8,128)(2,1)S(1)} %bitcast.29, bf16[32,40,256]{2,1,0:T(8,128)(2,1)S(1)} %collective-permute-done.5.right_ref), custom_call_target="tpu_custom_call" | custom-call | tf_op jit(solution)/shard_map/pallas_call | solution.py:63
  34.7 0.7 collective-permute-start.6
  35.4 48.4 %collective-permute-done.7 = bf16[8,40,256]{2,1,0:T(8,128)(2,1)S(1)} collective-permute-done((bf16[8,40,256]{2,1,0:T(8,128)(2,1)S(1)}, bf16[8,40,256]{2,1,0:T(8,128)(2,1)S(1)}, u32[]{:S(2)}, u32[]{:S(2)}) %collective-permute-start.7) | collective-permute-done | bytes 163872 | tf_op jit(solution)/shard_map/ppermute | solution.py:242
  83.8 0.1 maximum_select_fusion
  84.1 1.3 %collective-permute-start.11 = (bf16[24,40,256]{2,1,0:T(8,128)(2,1)S(1)}, bf16[24,40,256]{2,1,0:T(8,128)(2,1)S(1)}, u32[]{:S(2)}, u32[]{:S(2)}) collective-permute-start(bf16[24,40,256]{2,1,0:T(8,128)(2,1)S(1)} %get-tuple-element.39), channel_id=1, source_target_pairs={{0,16},{1,17},{2,18},{3,19},{4,20},{5,21},{6,22},{7,23},{8,24},{9,... | collective-permute-start | bytes 1474568 | tf_op jit(solution)/shard_map/ppermute | solution.py:161
  85.4 1.3 %collective-permute-start.12 = (bf16[24,40,256]{2,1,0:T(8,128)(2,1)S(1)}, bf16[24,40,256]{2,1,0:T(8,128)(2,1)S(1)}, u32[]{:S(2)}, u32[]{:S(2)}) collective-permute-start(bf16[24,40,256]{2,1,0:T(8,128)(2,1)S(1)} %get-tuple-element.40), channel_id=1, source_target_pairs={{16,0},{17,1},{18,2},{19,3},{20,4},{21,5},{22,6},{23,7},{24,8},{25... | collective-permute-start | bytes 1474568 | tf_op jit(solution)/shard_map/ppermute | solution.py:166
  86.7 0.2 select_reduce_fusion
  86.9 0.1 pad_maximum_fusion
  87.0 0.4 convolution_bitcast_fusion.1
  87.4 8.5 %collective-permute-done.11 = bf16[24,40,256]{2,1,0:T(8,128)(2,1)S(1)} collective-permute-done((bf16[24,40,256]{2,1,0:T(8,128)(2,1)S(1)}, bf16[24,40,256]{2,1,0:T(8,128)(2,1)S(1)}, u32[]{:S(2)}, u32[]{:S(2)}) %collective-permute-start.11) | collective-permute-done | bytes 491552 | tf_op jit(solution)/shard_map/ppermute | solution.py:161
  95.9 3.8 %collective-permute-done.12 = bf16[24,40,256]{2,1,0:T(8,128)(2,1)S(1)} collective-permute-done((bf16[24,40,256]{2,1,0:T(8,128)(2,1)S(1)}, bf16[24,40,256]{2,1,0:T(8,128)(2,1)S(1)}, u32[]{:S(2)}, u32[]{:S(2)}) %collective-permute-start.12) | collective-permute-done | bytes 491552 | tf_op jit(solution)/shard_map/ppermute | solution.py:166
  99.8 1.5 %fusion.1 = f32[40,32,256]{2,1,0:T(8,128)} fusion(f32[40,32,256]{2,1,0:T(8,128)S(1)} %convolution_bitcast_fusion.1, bf16[48,40,256]{2,1,0:T(8,128)(2,1)S(1)} %pad_maximum_fusion.1, f32[32]{0:T(128)S(1)} %sqrt.4, bf16[24,32]{0,1:T(8,128)(2,1)S(1)} %get-tuple-element.47, bf16[24,32]{0,1:T(8,128)(2,1)S(1)} %get-tuple-element.45), kind=kOutput, calls=%fused_computation.2 | convolution fusion | flops 32118784 | bytes 3607680 | tf_op jit(solution)/shard_map/jmc,jr->mrc/dot_general | solution.py:274
  (32 shorter events, 0.8 us)
Async XLA Ops:
  0.0 17.1 %copy-start = (s32[32]{0:T(128)S(1)}, s32[32]{0:T(128)}, u32[]{:S(2)}) copy-start(s32[32]{0:T(128)} %constant.106.clone) | copy-start | bytes 388
  1.5 24.5 %collective-permute-start.4 = (bf16[32,40,256]{2,1,0:T(8,128)(2,1)S(1)}, bf16[32,40,256]{2,1,0:T(8,128)(2,1)S(1)}, u32[]{:S(2)}, u32[]{:S(2)}) collective-permute-start(bf16[32,40,256]{2,1,0:T(8,128)(2,1)S(1)} %bitcast.25), channel_id=1, source_target_pairs={{32,33},{33,34},{34,35},{35,36},{36,37},{37,38},{38,39},{39,40},{4... | collective-permute-start | bytes 1966088 | tf_op jit(solution)/shard_map/ppermute | solution.py:220
  2.2 19.4 %collective-permute-start.1 = (bf16[8,40,256]{2,1,0:T(8,128)(2,1)S(1)}, bf16[8,40,256]{2,1,0:T(8,128)(2,1)S(1)}, u32[]{:S(2)}, u32[]{:S(2)}) collective-permute-start(bf16[8,40,256]{2,1,0:T(8,128)(2,1)S(1)} %get-tuple-element.41), channel_id=1, source_target_pairs={{0,160},{1,161},{2,162},{3,163},{4,164},{5,165},{6,166},{7,167},{8... | collective-permute-start | bytes 491528 | tf_op jit(solution)/shard_map/ppermute | solution.py:212
  12.1 10.3 %collective-permute-start.3 = (bf16[8,40,256]{2,1,0:T(8,128)(2,1)S(1)}, bf16[8,40,256]{2,1,0:T(8,128)(2,1)S(1)}, u32[]{:S(2)}, u32[]{:S(2)}) collective-permute-start(bf16[8,40,256]{2,1,0:T(8,128)(2,1)S(1)} %get-tuple-element.42), channel_id=1, source_target_pairs={{0,288},{1,289},{2,290},{3,291},{4,292},{5,293},{6,294},{7,295},{8... | collective-permute-start | bytes 491528 | tf_op jit(solution)/shard_map/ppermute | solution.py:212
  14.4 8.7 %collective-permute-start.2 = (bf16[8,40,256]{2,1,0:T(8,128)(2,1)S(1)}, bf16[8,40,256]{2,1,0:T(8,128)(2,1)S(1)}, u32[]{:S(2)}, u32[]{:S(2)}) collective-permute-start(bf16[8,40,256]{2,1,0:T(8,128)(2,1)S(1)} %get-tuple-element.43), channel_id=1, source_target_pairs={{0,416},{1,417},{2,418},{3,419},{4,420},{5,421},{6,422},{7,423},{8... | collective-permute-start | bytes 491528 | tf_op jit(solution)/shard_map/ppermute | solution.py:212
  15.7 9.9 %collective-permute-start = (bf16[8,40,256]{2,1,0:T(8,128)(2,1)S(1)}, bf16[8,40,256]{2,1,0:T(8,128)(2,1)S(1)}, u32[]{:S(2)}, u32[]{:S(2)}) collective-permute-start(bf16[8,40,256]{2,1,0:T(8,128)(2,1)S(1)} %get-tuple-element.44), channel_id=1, source_target_pairs={{0,32},{1,33},{2,34},{3,35},{4,36},{5,37},{6,38},{7,39},{8,40},{9,... | collective-permute-start | bytes 491528 | tf_op jit(solution)/shard_map/ppermute | solution.py:212
  21.6 4.3 %collective-permute-start.5 = (bf16[32,40,256]{2,1,0:T(8,128)(2,1)S(1)}, bf16[32,40,256]{2,1,0:T(8,128)(2,1)S(1)}, u32[]{:S(2)}, u32[]{:S(2)}) collective-permute-start(bf16[32,40,256]{2,1,0:T(8,128)(2,1)S(1)} %bitcast.27), channel_id=1, source_target_pairs={{32,47},{33,32},{34,33},{35,34},{36,35},{37,36},{38,37},{39,38},{4... | collective-permute-start | bytes 1966088 | tf_op jit(solution)/shard_map/ppermute | solution.py:223
  26.3 57.5 %collective-permute-start.10 = (bf16[8,40,256]{2,1,0:T(8,128)(2,1)S(1)}, bf16[8,40,256]{2,1,0:T(8,128)(2,1)S(1)}, u32[]{:S(2)}, u32[]{:S(2)}) collective-permute-start(bf16[8,40,256]{2,1,0:T(8,128)(2,1)S(1)} %reshape.72), channel_id=1, source_target_pairs={{208,496},{209,497},{210,498},{211,499},{212,500},{213,501},{214,5... | collective-permute-start | bytes 491528 | tf_op jit(solution)/shard_map/ppermute | solution.py:242
  27.6 56.3 %collective-permute-start.9 = (bf16[8,40,256]{2,1,0:T(8,128)(2,1)S(1)}, bf16[8,40,256]{2,1,0:T(8,128)(2,1)S(1)}, u32[]{:S(2)}, u32[]{:S(2)}) collective-permute-start(bf16[8,40,256]{2,1,0:T(8,128)(2,1)S(1)} %reshape.72), channel_id=1, source_target_pairs={{80,496},{81,497},{82,498},{83,499},{84,500},{85,501},{86,502},{87... | collective-permute-start | bytes 491528 | tf_op jit(solution)/shard_map/ppermute | solution.py:242
  28.9 55.0 %collective-permute-start.8 = (bf16[8,40,256]{2,1,0:T(8,128)(2,1)S(1)}, bf16[8,40,256]{2,1,0:T(8,128)(2,1)S(1)}, u32[]{:S(2)}, u32[]{:S(2)}) collective-permute-start(bf16[8,40,256]{2,1,0:T(8,128)(2,1)S(1)} %reshape.72), channel_id=1, source_target_pairs={{144,16},{145,17},{146,18},{147,19},{148,20},{149,21},{150,22},{15... | collective-permute-start | bytes 491528 | tf_op jit(solution)/shard_map/ppermute | solution.py:242
  30.2 53.6 %collective-permute-start.7 = (bf16[8,40,256]{2,1,0:T(8,128)(2,1)S(1)}, bf16[8,40,256]{2,1,0:T(8,128)(2,1)S(1)}, u32[]{:S(2)}, u32[]{:S(2)}) collective-permute-start(bf16[8,40,256]{2,1,0:T(8,128)(2,1)S(1)} %reshape.72), channel_id=1, source_target_pairs={{32,0},{33,1},{34,2},{35,3},{36,4},{37,5},{38,6},{39,7},{40,8},{41... | collective-permute-start | bytes 491528 | tf_op jit(solution)/shard_map/ppermute | solution.py:242
  34.7 52.2 %collective-permute-start.6 = (bf16[24,40,256]{2,1,0:T(8,128)(2,1)S(1)}, bf16[24,40,256]{2,1,0:T(8,128)(2,1)S(1)}, u32[]{:S(2)}, u32[]{:S(2)}) collective-permute-start(bf16[24,40,256]{2,1,0:T(8,128)(2,1)S(1)} %slice_select_fusion), channel_id=1, source_target_pairs={{48,64},{49,65},{50,66},{51,67},{52,68},{53,69},{54,70},{55,71},{5... | collective-permute-start | bytes 1474568 | tf_op jit(solution)/shard_map/ppermute | solution.py:154
  84.1 11.8 %collective-permute-start.11 = (bf16[24,40,256]{2,1,0:T(8,128)(2,1)S(1)}, bf16[24,40,256]{2,1,0:T(8,128)(2,1)S(1)}, u32[]{:S(2)}, u32[]{:S(2)}) collective-permute-start(bf16[24,40,256]{2,1,0:T(8,128)(2,1)S(1)} %get-tuple-element.39), channel_id=1, source_target_pairs={{0,16},{1,17},{2,18},{3,19},{4,20},{5,21},{6,22},{7,23},{8,24},{9,... | collective-permute-start | bytes 1474568 | tf_op jit(solution)/shard_map/ppermute | solution.py:161
  85.4 14.3 %collective-permute-start.12 = (bf16[24,40,256]{2,1,0:T(8,128)(2,1)S(1)}, bf16[24,40,256]{2,1,0:T(8,128)(2,1)S(1)}, u32[]{:S(2)}, u32[]{:S(2)}) collective-permute-start(bf16[24,40,256]{2,1,0:T(8,128)(2,1)S(1)} %get-tuple-element.40), channel_id=1, source_target_pairs={{16,0},{17,1},{18,2},{19,3},{20,4},{21,5},{22,6},{23,7},{24,8},{25... | collective-permute-start | bytes 1474568 | tf_op jit(solution)/shard_map/ppermute | solution.py:166

commit v7 on v6

--- a/solution.py
+++ b/solution.py
@@ -57,7 +57,7 @@
 
 def near_product(left, mid, right, widths, levels):
     rows, members, cols = mid.shape
-    step = 16
+    step = rows
     block = pl.BlockSpec((step, members, cols), lambda i: (i, 0, 0))
     smem = pl.BlockSpec(memory_space=pltpu.SMEM)
     return pl.pallas_call(

time: 102 us -> 102 us (level)
  no operation moved by 1% of the time
where the time goes in v7:
time: 102 us
  waiting for transfers between devices  64.6 us (63%)
  starting transfers between devices  24.7 us (24%)
  local copies, waits for them, and re-layouts  4.04 us (4%)
  Pallas kernels  2.95 us (3%)
  other arithmetic  1.93 us (2%)
  matrix products  1.88 us (2%)
  between operations  1.69 us (2%)
    ppermute x4, waiting for transfers between devices, body(): polar = [lax.ppermute(done, axes, pairs(returns(q))) for q in range(shares)]  48.9 us
    ppermute x4, starting transfers between devices, body(): lax.ppermute(data[q * share:(q + 1) * share], axes, pairs(hands(q)))  14.8 us
    ppermute x1, waiting for transfers between devices, next_halo(): lax.ppermute(along[-HALF_LAT:], axes, pairs(lambda lat, lon: (lat + 1, lo...  8.64 us
    ppermute x4, starting transfers between devices, body(): polar = [lax.ppermute(done, axes, pairs(returns(q))) for q in range(shares)]  5.17 us
    ppermute x1, waiting for transfers between devices, next_halo(): lax.ppermute(along[:HALF_LAT], axes, pairs(lambda lat, lon: (lat - 1, lon...  3.9 us
    ppermute x4, waiting for transfers between devices, body(): lax.ppermute(data[q * share:(q + 1) * share], axes, pairs(hands(q)))  3.17 us
    pallas_call x1, Pallas kernels, near_product(): pl.pallas_call(near_kernel, grid=(rows // step,), in_specs=[smem, smem, b...  2.95 us
  transfers between devices with their start and end apart: 13, of which 5 were waited for; matrix products, arithmetic and copies ran while one was open for 4% of the time, Pallas kernels for 3%

profile of v7, /device:TPU:1, one launch (start us, length us, event | category | flops | bytes accessed | tf_op | source)
XLA Modules:
  0.0 101.7 jit_solution(16831401844015655931)
XLA Ops:
  0.0 1.5 %copy.31 = bf16[40,32,256]{2,0,1:T(8,128)(2,1)S(1)} copy(bf16[40,32,256]{2,1,0:T(8,128)(2,1)} %param.5) | data formatting | bytes 1310720 | tf_op args[0]
  1.5 0.7 collective-permute-start.4
  2.2 9.9 %collective-permute-start.1 = (bf16[8,40,256]{2,1,0:T(8,128)(2,1)S(1)}, bf16[8,40,256]{2,1,0:T(8,128)(2,1)S(1)}, u32[]{:S(2)}, u32[]{:S(2)}) collective-permute-start(bf16[8,40,256]{2,1,0:T(8,128)(2,1)S(1)} %get-tuple-element.41), channel_id=1, source_target_pairs={{0,160},{1,161},{2,162},{3,163},{4,164},{5,165},{6,166},{7,167},{8... | collective-permute-start | bytes 491528 | tf_op jit(solution)/shard_map/ppermute | solution.py:212
  12.1 2.3 %collective-permute-start.3 = (bf16[8,40,256]{2,1,0:T(8,128)(2,1)S(1)}, bf16[8,40,256]{2,1,0:T(8,128)(2,1)S(1)}, u32[]{:S(2)}, u32[]{:S(2)}) collective-permute-start(bf16[8,40,256]{2,1,0:T(8,128)(2,1)S(1)} %get-tuple-element.42), channel_id=1, source_target_pairs={{0,288},{1,289},{2,290},{3,291},{4,292},{5,293},{6,294},{7,295},{8... | collective-permute-start | bytes 491528 | tf_op jit(solution)/shard_map/ppermute | solution.py:212
  14.4 1.3 %collective-permute-start.2 = (bf16[8,40,256]{2,1,0:T(8,128)(2,1)S(1)}, bf16[8,40,256]{2,1,0:T(8,128)(2,1)S(1)}, u32[]{:S(2)}, u32[]{:S(2)}) collective-permute-start(bf16[8,40,256]{2,1,0:T(8,128)(2,1)S(1)} %get-tuple-element.43), channel_id=1, source_target_pairs={{0,416},{1,417},{2,418},{3,419},{4,420},{5,421},{6,422},{7,423},{8... | collective-permute-start | bytes 491528 | tf_op jit(solution)/shard_map/ppermute | solution.py:212
  15.7 1.3 %collective-permute-start = (bf16[8,40,256]{2,1,0:T(8,128)(2,1)S(1)}, bf16[8,40,256]{2,1,0:T(8,128)(2,1)S(1)}, u32[]{:S(2)}, u32[]{:S(2)}) collective-permute-start(bf16[8,40,256]{2,1,0:T(8,128)(2,1)S(1)} %get-tuple-element.44), channel_id=1, source_target_pairs={{0,32},{1,33},{2,34},{3,35},{4,36},{5,37},{6,38},{7,39},{8,40},{9,... | collective-permute-start | bytes 491528 | tf_op jit(solution)/shard_map/ppermute | solution.py:212
  17.1 0.6 dynamic_slice.10
  18.4 0.8 dynamic-slice_convert_fusion.width_ref
  19.2 1.3 %dynamic_slice.11 = s32[1]{0:T(128)} dynamic-slice(s32[1024]{0:T(1024)} %param.6, s32[]{:T(128)S(6)} %select_n.86), dynamic_slice_sizes={1} | dynamic-slice | bytes 12 | tf_op jit(solution)/shard_map/dynamic_slice | solution.py:227
  21.3 0.3 fusion.6
  21.6 0.7 collective-permute-start.5
  22.5 0.7 collective-permute-done.2
  23.2 2.5 %collective-permute-done = bf16[8,40,256]{2,1,0:T(8,128)(2,1)S(1)} collective-permute-done((bf16[8,40,256]{2,1,0:T(8,128)(2,1)S(1)}, bf16[8,40,256]{2,1,0:T(8,128)(2,1)S(1)}, u32[]{:S(2)}, u32[]{:S(2)}) %collective-permute-start) | collective-permute-done | bytes 163872 | tf_op jit(solution)/shard_map/ppermute | solution.py:212
  25.7 0.1 copy.18
  26.0 0.2 copy.22
  26.2 0.1 reshape.72
  26.3 1.3 %collective-permute-start.10 = (bf16[8,40,256]{2,1,0:T(8,128)(2,1)S(1)}, bf16[8,40,256]{2,1,0:T(8,128)(2,1)S(1)}, u32[]{:S(2)}, u32[]{:S(2)}) collective-permute-start(bf16[8,40,256]{2,1,0:T(8,128)(2,1)S(1)} %reshape.72), channel_id=1, source_target_pairs={{208,496},{209,497},{210,498},{211,499},{212,500},{213,501},{214,5... | collective-permute-start | bytes 491528 | tf_op jit(solution)/shard_map/ppermute | solution.py:242
  27.6 1.3 %collective-permute-start.9 = (bf16[8,40,256]{2,1,0:T(8,128)(2,1)S(1)}, bf16[8,40,256]{2,1,0:T(8,128)(2,1)S(1)}, u32[]{:S(2)}, u32[]{:S(2)}) collective-permute-start(bf16[8,40,256]{2,1,0:T(8,128)(2,1)S(1)} %reshape.72), channel_id=1, source_target_pairs={{80,496},{81,497},{82,498},{83,499},{84,500},{85,501},{86,502},{87... | collective-permute-start | bytes 491528 | tf_op jit(solution)/shard_map/ppermute | solution.py:242
  28.9 1.3 %collective-permute-start.8 = (bf16[8,40,256]{2,1,0:T(8,128)(2,1)S(1)}, bf16[8,40,256]{2,1,0:T(8,128)(2,1)S(1)}, u32[]{:S(2)}, u32[]{:S(2)}) collective-permute-start(bf16[8,40,256]{2,1,0:T(8,128)(2,1)S(1)} %reshape.72), channel_id=1, source_target_pairs={{144,16},{145,17},{146,18},{147,19},{148,20},{149,21},{150,22},{15... | collective-permute-start | bytes 491528 | tf_op jit(solution)/shard_map/ppermute | solution.py:242
  30.2 1.3 %collective-permute-start.7 = (bf16[8,40,256]{2,1,0:T(8,128)(2,1)S(1)}, bf16[8,40,256]{2,1,0:T(8,128)(2,1)S(1)}, u32[]{:S(2)}, u32[]{:S(2)}) collective-permute-start(bf16[8,40,256]{2,1,0:T(8,128)(2,1)S(1)} %reshape.72), channel_id=1, source_target_pairs={{32,0},{33,1},{34,2},{35,3},{36,4},{37,5},{38,6},{39,7},{40,8},{41... | collective-permute-start | bytes 491528 | tf_op jit(solution)/shard_map/ppermute | solution.py:242
  31.5 2.9 %shard_map.37 = bf16[32,40,256]{2,1,0:T(8,128)(2,1)S(1)} custom-call(f32[32]{0:T(128)S(1)} %dynamic-slice_convert_fusion.width_ref, f32[32]{0:T(128)S(1)} %bitcast.33, bf16[32,40,256]{2,1,0:T(8,128)(2,1)S(1)} %collective-permute-done.4.left_ref, bf16[32,40,256]{2,1,0:T(8,128)(2,1)S(1)} %bitcast.29, bf16[32,40,256]{2,1,0:T(8,128)(2,1)S(1)} %collective-permute-done.5.right_ref), custom_call_target="tpu_custom_call" | custom-call | tf_op jit(solution)/shard_map/pallas_call | solution.py:63
  34.5 0.7 collective-permute-start.6
  35.2 48.9 %collective-permute-done.7 = bf16[8,40,256]{2,1,0:T(8,128)(2,1)S(1)} collective-permute-done((bf16[8,40,256]{2,1,0:T(8,128)(2,1)S(1)}, bf16[8,40,256]{2,1,0:T(8,128)(2,1)S(1)}, u32[]{:S(2)}, u32[]{:S(2)}) %collective-permute-start.7) | collective-permute-done | bytes 163872 | tf_op jit(solution)/shard_map/ppermute | solution.py:242
  84.1 0.1 maximum_select_fusion
  84.3 1.3 %collective-permute-start.11 = (bf16[24,40,256]{2,1,0:T(8,128)(2,1)S(1)}, bf16[24,40,256]{2,1,0:T(8,128)(2,1)S(1)}, u32[]{:S(2)}, u32[]{:S(2)}) collective-permute-start(bf16[24,40,256]{2,1,0:T(8,128)(2,1)S(1)} %get-tuple-element.39), channel_id=1, source_target_pairs={{0,16},{1,17},{2,18},{3,19},{4,20},{5,21},{6,22},{7,23},{8,24},{9,... | collective-permute-start | bytes 1474568 | tf_op jit(solution)/shard_map/ppermute | solution.py:161
  85.6 1.3 %collective-permute-start.12 = (bf16[24,40,256]{2,1,0:T(8,128)(2,1)S(1)}, bf16[24,40,256]{2,1,0:T(8,128)(2,1)S(1)}, u32[]{:S(2)}, u32[]{:S(2)}) collective-permute-start(bf16[24,40,256]{2,1,0:T(8,128)(2,1)S(1)} %get-tuple-element.40), channel_id=1, source_target_pairs={{16,0},{17,1},{18,2},{19,3},{20,4},{21,5},{22,6},{23,7},{24,8},{25... | collective-permute-start | bytes 1474568 | tf_op jit(solution)/shard_map/ppermute | solution.py:166
  86.9 0.2 select_reduce_fusion
  87.1 0.1 pad_maximum_fusion
  87.2 0.4 convolution_bitcast_fusion.1
  87.7 8.6 %collective-permute-done.11 = bf16[24,40,256]{2,1,0:T(8,128)(2,1)S(1)} collective-permute-done((bf16[24,40,256]{2,1,0:T(8,128)(2,1)S(1)}, bf16[24,40,256]{2,1,0:T(8,128)(2,1)S(1)}, u32[]{:S(2)}, u32[]{:S(2)}) %collective-permute-start.11) | collective-permute-done | bytes 491552 | tf_op jit(solution)/shard_map/ppermute | solution.py:161
  96.3 3.9 %collective-permute-done.12 = bf16[24,40,256]{2,1,0:T(8,128)(2,1)S(1)} collective-permute-done((bf16[24,40,256]{2,1,0:T(8,128)(2,1)S(1)}, bf16[24,40,256]{2,1,0:T(8,128)(2,1)S(1)}, u32[]{:S(2)}, u32[]{:S(2)}) %collective-permute-start.12) | collective-permute-done | bytes 491552 | tf_op jit(solution)/shard_map/ppermute | solution.py:166
  100.3 1.5 %fusion.1 = f32[40,32,256]{2,1,0:T(8,128)} fusion(f32[40,32,256]{2,1,0:T(8,128)S(1)} %convolution_bitcast_fusion.1, bf16[48,40,256]{2,1,0:T(8,128)(2,1)S(1)} %pad_maximum_fusion.1, f32[32]{0:T(128)S(1)} %sqrt.4, bf16[24,32]{0,1:T(8,128)(2,1)S(1)} %get-tuple-element.47, bf16[24,32]{0,1:T(8,128)(2,1)S(1)} %get-tuple-element.45), kind=kOutput, calls=%fused_computation.2 | convolution fusion | flops 32118784 | bytes 3607680 | tf_op jit(solution)/shard_map/jmc,jr->mrc/dot_general | solution.py:274
  (32 shorter events, 0.8 us)
Async XLA Ops:
  0.0 17.1 %copy-start = (s32[32]{0:T(128)S(1)}, s32[32]{0:T(128)}, u32[]{:S(2)}) copy-start(s32[32]{0:T(128)} %constant.106.clone) | copy-start | bytes 388
  1.5 24.5 %collective-permute-start.4 = (bf16[32,40,256]{2,1,0:T(8,128)(2,1)S(1)}, bf16[32,40,256]{2,1,0:T(8,128)(2,1)S(1)}, u32[]{:S(2)}, u32[]{:S(2)}) collective-permute-start(bf16[32,40,256]{2,1,0:T(8,128)(2,1)S(1)} %bitcast.25), channel_id=1, source_target_pairs={{32,33},{33,34},{34,35},{35,36},{36,37},{37,38},{38,39},{39,40},{4... | collective-permute-start | bytes 1966088 | tf_op jit(solution)/shard_map/ppermute | solution.py:220
  2.2 19.4 %collective-permute-start.1 = (bf16[8,40,256]{2,1,0:T(8,128)(2,1)S(1)}, bf16[8,40,256]{2,1,0:T(8,128)(2,1)S(1)}, u32[]{:S(2)}, u32[]{:S(2)}) collective-permute-start(bf16[8,40,256]{2,1,0:T(8,128)(2,1)S(1)} %get-tuple-element.41), channel_id=1, source_target_pairs={{0,160},{1,161},{2,162},{3,163},{4,164},{5,165},{6,166},{7,167},{8... | collective-permute-start | bytes 491528 | tf_op jit(solution)/shard_map/ppermute | solution.py:212
  12.1 10.3 %collective-permute-start.3 = (bf16[8,40,256]{2,1,0:T(8,128)(2,1)S(1)}, bf16[8,40,256]{2,1,0:T(8,128)(2,1)S(1)}, u32[]{:S(2)}, u32[]{:S(2)}) collective-permute-start(bf16[8,40,256]{2,1,0:T(8,128)(2,1)S(1)} %get-tuple-element.42), channel_id=1, source_target_pairs={{0,288},{1,289},{2,290},{3,291},{4,292},{5,293},{6,294},{7,295},{8... | collective-permute-start | bytes 491528 | tf_op jit(solution)/shard_map/ppermute | solution.py:212
  14.4 8.7 %collective-permute-start.2 = (bf16[8,40,256]{2,1,0:T(8,128)(2,1)S(1)}, bf16[8,40,256]{2,1,0:T(8,128)(2,1)S(1)}, u32[]{:S(2)}, u32[]{:S(2)}) collective-permute-start(bf16[8,40,256]{2,1,0:T(8,128)(2,1)S(1)} %get-tuple-element.43), channel_id=1, source_target_pairs={{0,416},{1,417},{2,418},{3,419},{4,420},{5,421},{6,422},{7,423},{8... | collective-permute-start | bytes 491528 | tf_op jit(solution)/shard_map/ppermute | solution.py:212
  15.7 9.9 %collective-permute-start = (bf16[8,40,256]{2,1,0:T(8,128)(2,1)S(1)}, bf16[8,40,256]{2,1,0:T(8,128)(2,1)S(1)}, u32[]{:S(2)}, u32[]{:S(2)}) collective-permute-start(bf16[8,40,256]{2,1,0:T(8,128)(2,1)S(1)} %get-tuple-element.44), channel_id=1, source_target_pairs={{0,32},{1,33},{2,34},{3,35},{4,36},{5,37},{6,38},{7,39},{8,40},{9,... | collective-permute-start | bytes 491528 | tf_op jit(solution)/shard_map/ppermute | solution.py:212
  21.6 4.3 %collective-permute-start.5 = (bf16[32,40,256]{2,1,0:T(8,128)(2,1)S(1)}, bf16[32,40,256]{2,1,0:T(8,128)(2,1)S(1)}, u32[]{:S(2)}, u32[]{:S(2)}) collective-permute-start(bf16[32,40,256]{2,1,0:T(8,128)(2,1)S(1)} %bitcast.27), channel_id=1, source_target_pairs={{32,47},{33,32},{34,33},{35,34},{36,35},{37,36},{38,37},{39,38},{4... | collective-permute-start | bytes 1966088 | tf_op jit(solution)/shard_map/ppermute | solution.py:223
  26.3 57.8 %collective-permute-start.10 = (bf16[8,40,256]{2,1,0:T(8,128)(2,1)S(1)}, bf16[8,40,256]{2,1,0:T(8,128)(2,1)S(1)}, u32[]{:S(2)}, u32[]{:S(2)}) collective-permute-start(bf16[8,40,256]{2,1,0:T(8,128)(2,1)S(1)} %reshape.72), channel_id=1, source_target_pairs={{208,496},{209,497},{210,498},{211,499},{212,500},{213,501},{214,5... | collective-permute-start | bytes 491528 | tf_op jit(solution)/shard_map/ppermute | solution.py:242
  27.6 56.5 %collective-permute-start.9 = (bf16[8,40,256]{2,1,0:T(8,128)(2,1)S(1)}, bf16[8,40,256]{2,1,0:T(8,128)(2,1)S(1)}, u32[]{:S(2)}, u32[]{:S(2)}) collective-permute-start(bf16[8,40,256]{2,1,0:T(8,128)(2,1)S(1)} %reshape.72), channel_id=1, source_target_pairs={{80,496},{81,497},{82,498},{83,499},{84,500},{85,501},{86,502},{87... | collective-permute-start | bytes 491528 | tf_op jit(solution)/shard_map/ppermute | solution.py:242
  28.9 55.2 %collective-permute-start.8 = (bf16[8,40,256]{2,1,0:T(8,128)(2,1)S(1)}, bf16[8,40,256]{2,1,0:T(8,128)(2,1)S(1)}, u32[]{:S(2)}, u32[]{:S(2)}) collective-permute-start(bf16[8,40,256]{2,1,0:T(8,128)(2,1)S(1)} %reshape.72), channel_id=1, source_target_pairs={{144,16},{145,17},{146,18},{147,19},{148,20},{149,21},{150,22},{15... | collective-permute-start | bytes 491528 | tf_op jit(solution)/shard_map/ppermute | solution.py:242
  30.2 53.9 %collective-permute-start.7 = (bf16[8,40,256]{2,1,0:T(8,128)(2,1)S(1)}, bf16[8,40,256]{2,1,0:T(8,128)(2,1)S(1)}, u32[]{:S(2)}, u32[]{:S(2)}) collective-permute-start(bf16[8,40,256]{2,1,0:T(8,128)(2,1)S(1)} %reshape.72), channel_id=1, source_target_pairs={{32,0},{33,1},{34,2},{35,3},{36,4},{37,5},{38,6},{39,7},{40,8},{41... | collective-permute-start | bytes 491528 | tf_op jit(solution)/shard_map/ppermute | solution.py:242
  34.5 52.6 %collective-permute-start.6 = (bf16[24,40,256]{2,1,0:T(8,128)(2,1)S(1)}, bf16[24,40,256]{2,1,0:T(8,128)(2,1)S(1)}, u32[]{:S(2)}, u32[]{:S(2)}) collective-permute-start(bf16[24,40,256]{2,1,0:T(8,128)(2,1)S(1)} %slice_select_fusion), channel_id=1, source_target_pairs={{48,64},{49,65},{50,66},{51,67},{52,68},{53,69},{54,70},{55,71},{5... | collective-permute-start | bytes 1474568 | tf_op jit(solution)/shard_map/ppermute | solution.py:154
  84.3 12.0 %collective-permute-start.11 = (bf16[24,40,256]{2,1,0:T(8,128)(2,1)S(1)}, bf16[24,40,256]{2,1,0:T(8,128)(2,1)S(1)}, u32[]{:S(2)}, u32[]{:S(2)}) collective-permute-start(bf16[24,40,256]{2,1,0:T(8,128)(2,1)S(1)} %get-tuple-element.39), channel_id=1, source_target_pairs={{0,16},{1,17},{2,18},{3,19},{4,20},{5,21},{6,22},{7,23},{8,24},{9,... | collective-permute-start | bytes 1474568 | tf_op jit(solution)/shard_map/ppermute | solution.py:161
  85.6 14.6 %collective-permute-start.12 = (bf16[24,40,256]{2,1,0:T(8,128)(2,1)S(1)}, bf16[24,40,256]{2,1,0:T(8,128)(2,1)S(1)}, u32[]{:S(2)}, u32[]{:S(2)}) collective-permute-start(bf16[24,40,256]{2,1,0:T(8,128)(2,1)S(1)} %get-tuple-element.40), channel_id=1, source_target_pairs={{16,0},{17,1},{18,2},{19,3},{20,4},{21,5},{22,6},{23,7},{24,8},{25... | collective-permute-start | bytes 1474568 | tf_op jit(solution)/shard_map/ppermute | solution.py:166
